TPU v7x, 32 devices: a whole 2x2x4 slice. The times are simulated.
32 devices in a mesh: dp: 8 (over z, y), fsdp: 4 (over x, core).
Axes of the slice: x: 2, y: 2, z: 4, core: 2. Of those that a mesh axis runs over, the one named last changes fastest.
Arguments:
- hidden: bfloat16 [2, 32, 256, 768], P(None, ('dp', 'fsdp')), may hold values from -6 to 6, as said below
- memory: bfloat16 [2, 32, 256, 768], P(None, ('dp', 'fsdp')), may hold values from -6 to 6, as said below
- cotangent: bfloat16 [2, 32, 256, 768], P(None, ('dp', 'fsdp')), may hold values from -6 to 6, as said below
- target_lengths: int32 [2, 32], P(None, ('dp', 'fsdp')), may hold values from 64 to 256, as said below
- memory_lengths: int32 [2, 32], P(None, ('dp', 'fsdp')), may hold values from 64 to 256, as said below
- qk_master: float32 [4, 768, 768], P(None, ('dp', 'fsdp')), may hold values from -0.21875 to 0.21875
- value_master: float32 [2, 768, 768], P(None, ('dp', 'fsdp')), may hold values from -0.21875 to 0.21875
- output_master: float32 [2, 768, 768], P(None, ('dp', 'fsdp')), may hold values from -1.25 to 1.25
- inner_master: float32 [768, 3072], P(('dp', 'fsdp')), may hold values from -0.21875 to 0.21875
- outer_master: float32 [3072, 768], P(('dp', 'fsdp')), may hold values from -0.109375 to 0.109375
- gain_master: float32 [3, 768], P(None, ('dp', 'fsdp')), may hold values from 0.5 to 1.5
- table_master: float32 [32, 12], replicated, may hold values from -6 to 6
- qk_first: float32 [4, 768, 768], P(None, ('dp', 'fsdp')), may hold values from -40 to 40
- value_first: float32 [2, 768, 768], P(None, ('dp', 'fsdp')), may hold values from -160 to 160
- output_first: float32 [2, 768, 768], P(None, ('dp', 'fsdp')), may hold values from -12 to 12
- inner_first: float32 [768, 3072], P(('dp', 'fsdp')), may hold values from -12 to 12
- outer_first: float32 [3072, 768], P(('dp', 'fsdp')), may hold values from -32 to 32
- gain_first: float32 [3, 768], P(None, ('dp', 'fsdp')), may hold values from -80 to 80
- table_first: float32 [32, 12], replicated, may hold values from -64 to 64
- qk_second: float32 [4, 768, 768], P(None, ('dp', 'fsdp')), may hold values from 2.048 to 32.768
- value_second: float32 [2, 768, 768], P(None, ('dp', 'fsdp')), may hold values from 32.768 to 524.288
- output_second: float32 [2, 768, 768], P(None, ('dp', 'fsdp')), may hold values from 0.18432 to 2.94912
- inner_second: float32 [768, 3072], P(('dp', 'fsdp')), may hold values from 0.18432 to 2.94912
- outer_second: float32 [3072, 768], P(('dp', 'fsdp')), may hold values from 1.31072 to 20.97152
- gain_second: float32 [3, 768], P(None, ('dp', 'fsdp')), may hold values from 8.192 to 131.072
- table_second: float32 [32, 12], replicated, may hold values from 5.89824 to 94.37184
Outputs:
- layer_out: bfloat16 [2, 32, 256, 768], P(None, ('dp', 'fsdp'))
- hidden_grad: float32 [2, 32, 256, 768], P(None, ('dp', 'fsdp'))
- memory_grad: float32 [2, 32, 256, 768], P(None, ('dp', 'fsdp'))
- qk_new: float32 [4, 768, 768], P(None, ('dp', 'fsdp'))
- value_new: float32 [2, 768, 768], P(None, ('dp', 'fsdp'))
- output_new: float32 [2, 768, 768], P(None, ('dp', 'fsdp'))
- inner_new: float32 [768, 3072], P(('dp', 'fsdp'))
- outer_new: float32 [3072, 768], P(('dp', 'fsdp'))
- gain_new: float32 [3, 768], P(None, ('dp', 'fsdp'))
- table_new: float32 [32, 12], replicated
- qk_first_new: float32 [4, 768, 768], P(None, ('dp', 'fsdp'))
- value_first_new: float32 [2, 768, 768], P(None, ('dp', 'fsdp'))
- output_first_new: float32 [2, 768, 768], P(None, ('dp', 'fsdp'))
- inner_first_new: float32 [768, 3072], P(('dp', 'fsdp'))
- outer_first_new: float32 [3072, 768], P(('dp', 'fsdp'))
- gain_first_new: float32 [3, 768], P(None, ('dp', 'fsdp'))
- table_first_new: float32 [32, 12], replicated
- qk_second_new: float32 [4, 768, 768], P(None, ('dp', 'fsdp'))
- value_second_new: float32 [2, 768, 768], P(None, ('dp', 'fsdp'))
- output_second_new: float32 [2, 768, 768], P(None, ('dp', 'fsdp'))
- inner_second_new: float32 [768, 3072], P(('dp', 'fsdp'))
- outer_second_new: float32 [3072, 768], P(('dp', 'fsdp'))
- gain_second_new: float32 [3, 768], P(None, ('dp', 'fsdp'))
- table_second_new: float32 [32, 12], replicated
- qk_copy: bfloat16 [4, 768, 768], P(None, ('dp', 'fsdp'))
- value_copy: bfloat16 [2, 768, 768], P(None, ('dp', 'fsdp'))
- output_copy: bfloat16 [2, 768, 768], P(None, ('dp', 'fsdp'))
- inner_copy: bfloat16 [768, 3072], P(('dp', 'fsdp'))
- outer_copy: bfloat16 [3072, 768], P(('dp', 'fsdp'))
- gain_copy: bfloat16 [3, 768], P(None, ('dp', 'fsdp'))
- table_copy: bfloat16 [32, 12], replicated
Inputs may be any that keep to these rules, and one draw needn't show every extreme that they name: `target_lengths`: each is at least 64, and some sequence has exactly 256. `memory_lengths`: each is at least 64, and some sequence has exactly 256. `hidden`: independent entries of mean 0 and deviation 1. `memory`: independent entries of mean 0 and deviation 1. `cotangent`: independent entries of mean 0 and deviation 1.
All inputs are finite; a program needn't handle non-finite values.
Results may differ from a plain program's by a relative error of at most 0.015.
The roundings to bfloat16 on the way count: a program that leaves them out, or rounds other values in their place, can miss the bound.
Values may be sent and summed in bfloat16 or wider, within the bound.
A program may use at most 256 MiB of HBM per device.

v0:
```python
import math

import jax
import jax.numpy as jnp
from jax import lax
from jax.sharding import PartitionSpec as P

HEADS = 12
HEAD_DIM = 64
BUCKETS = 32
MAX_DIST = 128
STEP = 10


epsilon_norm = 1e-06
score_scale = 0.125
masked_score = -1e30
beta_first = 0.9
beta_second = 0.999
adam_epsilon = 1e-08
rate_matrix = 0.15
rate_small = 1.0
weight_decay = 0.01
highest = lax.Precision.HIGHEST


def bucket_onehot(length):
    places = jnp.arange(length, dtype=jnp.int32)
    distance = jnp.maximum(places[:, None] - places[None, :], 0)
    exact_range = BUCKETS // 2
    safe_distance = jnp.maximum(distance, 1).astype(jnp.float32)
    spread = (
        jnp.log(safe_distance / exact_range)
        / math.log(MAX_DIST / exact_range)
        * (BUCKETS - exact_range)
    )
    far_bucket = jnp.minimum(exact_range + spread.astype(jnp.int32), BUCKETS - 1)
    bucket = jnp.where(distance < exact_range, distance, far_bucket)
    labels = jnp.arange(BUCKETS, dtype=jnp.int32)
    return (bucket[None, :, :] == labels[:, None, None]).astype(jnp.float32)


def product(left_side, right_side):
    return jnp.dot(left_side, right_side, preferred_element_type=jnp.float32)


def product_over_rows(left_side, right_side):
    return lax.dot_general(
        left_side, right_side, (((0,), (0,)), ((), ())), preferred_element_type=jnp.float32
    )


def product_transposed(left_side, right_side):
    return lax.dot_general(
        left_side, right_side, (((1,), (1,)), ((), ())), preferred_element_type=jnp.float32
    )


def to_heads(values, sequences):
    return values.reshape(sequences, -1, HEADS, HEAD_DIM)


def normalize(values, gain_row):
    scale_rows = lax.rsqrt(jnp.mean(values * values, axis=-1, keepdims=True) + epsilon_norm)
    unit_rows = values * scale_rows
    return ((unit_rows * gain_row).astype(jnp.bfloat16), unit_rows, scale_rows)


def normalize_back(grad_norm, unit_rows, scale_rows, gain_row):
    gain_grad = jnp.sum(grad_norm * unit_rows, axis=0)
    grad_unit = grad_norm * gain_row
    grad_values = scale_rows * (
        grad_unit - unit_rows * jnp.mean(grad_unit * unit_rows, axis=-1, keepdims=True)
    )
    return (grad_values, gain_grad)


def attend_scores(queries, key_heads, bias_term, allowed):
    scores = (
        jnp.einsum("sihe,sjhe->shij", queries, key_heads, preferred_element_type=jnp.float32)
        * score_scale
        + bias_term
    )
    return jnp.where(allowed, scores, masked_score)


def attend_forward(queries, key_heads, value_heads, bias_term, allowed):
    scores = attend_scores(queries, key_heads, bias_term, allowed)
    row_max = jnp.max(scores, axis=-1, keepdims=True)
    expanded = jnp.exp(scores - row_max)
    row_total = jnp.sum(expanded, axis=-1, keepdims=True)
    weights = (expanded / row_total).astype(jnp.bfloat16)
    mixed_heads = jnp.einsum(
        "shij,sjhe->sihe", weights, value_heads, preferred_element_type=jnp.float32
    )
    return (mixed_heads, row_max + jnp.log(row_total))


def attend_back(queries, key_heads, value_heads, bias_term, allowed, summary, grad_mixed):
    scores = attend_scores(queries, key_heads, bias_term, allowed)
    weights = jnp.exp(scores - summary)
    grad_weights = jnp.einsum(
        "sihe,sjhe->shij", grad_mixed, value_heads, preferred_element_type=jnp.float32
    )
    grad_values = jnp.einsum(
        "shij,sihe->sjhe",
        weights.astype(jnp.bfloat16),
        grad_mixed,
        preferred_element_type=jnp.float32,
    )
    grad_scores = (
        weights * (grad_weights - jnp.sum(weights * grad_weights, axis=-1, keepdims=True))
    ).astype(jnp.bfloat16)
    grad_queries = (
        jnp.einsum("shij,sjhe->sihe", grad_scores, key_heads, preferred_element_type=jnp.float32)
        * score_scale
    )
    grad_keys = (
        jnp.einsum("shij,sihe->sjhe", grad_scores, queries, preferred_element_type=jnp.float32)
        * score_scale
    )
    return (grad_queries, grad_keys, grad_values, grad_scores)


def forward_pass(gathered, bias_heads, hidden_seq, memory_seq, target_len, memory_len):
    qk_full, value_full, output_full, inner_full, outer_full, gain_full = gathered
    gain_rows = gain_full.astype(jnp.float32)
    sequences, length, model_width = hidden_seq.shape
    memory_span = memory_seq.shape[1]
    row_count = sequences * length
    residual = hidden_seq.astype(jnp.float32).reshape(row_count, model_width)
    memory_rows = memory_seq.reshape(sequences * memory_span, model_width)
    places = jnp.arange(length, dtype=jnp.int32)
    self_mask = (places[None, :] <= places[:, None])[None, None] & (
        places[None, None, None, :] < target_len[:, None, None, None]
    )
    memory_places = jnp.arange(memory_span, dtype=jnp.int32)
    cross_mask = (memory_places[None, :] < memory_len[:, None])[:, None, None, :]
    normed_first, unit_first, scale_first = normalize(residual, gain_rows[0])
    query_first = product(normed_first, qk_full[0]).astype(jnp.bfloat16)
    key_first = product(normed_first, qk_full[1]).astype(jnp.bfloat16)
    value_first = product(normed_first, value_full[0]).astype(jnp.bfloat16)
    mixed_first, summary_first = attend_forward(
        to_heads(query_first, sequences),
        to_heads(key_first, sequences),
        to_heads(value_first, sequences),
        bias_heads,
        self_mask,
    )
    mixed_first = mixed_first.reshape(row_count, model_width).astype(jnp.bfloat16)
    first_sum = residual + product(mixed_first, output_full[0])
    normed_second, unit_second, scale_second = normalize(first_sum, gain_rows[1])
    query_second = product(normed_second, qk_full[2]).astype(jnp.bfloat16)
    key_second = product(memory_rows, qk_full[3]).astype(jnp.bfloat16)
    value_second = product(memory_rows, value_full[1]).astype(jnp.bfloat16)
    mixed_second, summary_second = attend_forward(
        to_heads(query_second, sequences),
        to_heads(key_second, sequences),
        to_heads(value_second, sequences),
        0.0,
        cross_mask,
    )
    mixed_second = mixed_second.reshape(row_count, model_width).astype(jnp.bfloat16)
    second_sum = first_sum + product(mixed_second, output_full[1])
    normed_third, unit_third, scale_third = normalize(second_sum, gain_rows[2])
    inner_act = product(normed_third, inner_full)
    activated = jax.nn.gelu(inner_act, approximate=True).astype(jnp.bfloat16)
    produced = (second_sum + product(activated, outer_full)).astype(jnp.bfloat16)
    stored = (
        self_mask,
        cross_mask,
        memory_rows,
        normed_first,
        unit_first,
        scale_first,
        query_first,
        key_first,
        value_first,
        summary_first,
        mixed_first,
        normed_second,
        unit_second,
        scale_second,
        query_second,
        key_second,
        value_second,
        summary_second,
        mixed_second,
        normed_third,
        unit_third,
        scale_third,
        inner_act,
        activated,
    )
    return (stored, produced.reshape(sequences, length, model_width))


def backward_pass(gathered, bias_heads, stored, cotangent_seq, target_len):
    qk_full, value_full, output_full, inner_full, outer_full, gain_full = gathered
    gain_rows = gain_full.astype(jnp.float32)
    (
        self_mask,
        cross_mask,
        memory_rows,
        normed_first,
        unit_first,
        scale_first,
        query_first,
        key_first,
        value_first,
        summary_first,
        mixed_first,
        normed_second,
        unit_second,
        scale_second,
        query_second,
        key_second,
        value_second,
        summary_second,
        mixed_second,
        normed_third,
        unit_third,
        scale_third,
        inner_act,
        activated,
    ) = stored
    sequences, length, model_width = cotangent_seq.shape
    row_count = sequences * length
    places = jnp.arange(length, dtype=jnp.int32)
    live_rows = (places[None, :] < target_len[:, None]).astype(jnp.float32).reshape(row_count, 1)
    grad_out = cotangent_seq.astype(jnp.float32).reshape(row_count, model_width) * live_rows
    branch = grad_out.astype(jnp.bfloat16)
    outer_grad = product_over_rows(activated, branch)
    grad_act = product_transposed(branch, outer_full)
    unused_value, gelu_pull = jax.vjp(
        lambda inputs: jax.nn.gelu(inputs, approximate=True), inner_act
    )
    grad_inner = gelu_pull(grad_act)[0].astype(jnp.bfloat16)
    inner_grad = product_over_rows(normed_third, grad_inner)
    grad_from_third, gain_third = normalize_back(
        product_transposed(grad_inner, inner_full), unit_third, scale_third, gain_rows[2]
    )
    grad_second = grad_out + grad_from_third
    branch = grad_second.astype(jnp.bfloat16)
    output_grad_second = product_over_rows(mixed_second, branch)
    grad_mixed = product_transposed(branch, output_full[1]).astype(jnp.bfloat16)
    grad_query, grad_key, grad_value, unused_scores = attend_back(
        to_heads(query_second, sequences),
        to_heads(key_second, sequences),
        to_heads(value_second, sequences),
        0.0,
        cross_mask,
        summary_second,
        to_heads(grad_mixed, sequences),
    )
    grad_query = grad_query.reshape(row_count, model_width).astype(jnp.bfloat16)
    grad_key = grad_key.reshape(memory_rows.shape[0], model_width).astype(jnp.bfloat16)
    grad_value = grad_value.reshape(memory_rows.shape[0], model_width).astype(jnp.bfloat16)
    qk_grad_two = product_over_rows(normed_second, grad_query)
    qk_grad_three = product_over_rows(memory_rows, grad_key)
    value_grad_one = product_over_rows(memory_rows, grad_value)
    memory_grad = product_transposed(grad_key, qk_full[3]) + product_transposed(
        grad_value, value_full[1]
    )
    grad_from_second, gain_second = normalize_back(
        product_transposed(grad_query, qk_full[2]), unit_second, scale_second, gain_rows[1]
    )
    grad_first = grad_second + grad_from_second
    branch = grad_first.astype(jnp.bfloat16)
    output_grad_first = product_over_rows(mixed_first, branch)
    grad_mixed = product_transposed(branch, output_full[0]).astype(jnp.bfloat16)
    grad_query, grad_key, grad_value, grad_scores = attend_back(
        to_heads(query_first, sequences),
        to_heads(key_first, sequences),
        to_heads(value_first, sequences),
        bias_heads,
        self_mask,
        summary_first,
        to_heads(grad_mixed, sequences),
    )
    grad_query = grad_query.reshape(row_count, model_width).astype(jnp.bfloat16)
    grad_key = grad_key.reshape(row_count, model_width).astype(jnp.bfloat16)
    grad_value = grad_value.reshape(row_count, model_width).astype(jnp.bfloat16)
    qk_grad_zero = product_over_rows(normed_first, grad_query)
    qk_grad_one = product_over_rows(normed_first, grad_key)
    value_grad_zero = product_over_rows(normed_first, grad_value)
    grad_norm = (
        product_transposed(grad_query, qk_full[0])
        + product_transposed(grad_key, qk_full[1])
        + product_transposed(grad_value, value_full[0])
    )
    grad_from_first, gain_first = normalize_back(grad_norm, unit_first, scale_first, gain_rows[0])
    hidden_grad = grad_first + grad_from_first
    score_term = jnp.sum(grad_scores.astype(jnp.float32), axis=0)
    grad_terms = (
        jnp.stack([qk_grad_zero, qk_grad_one, qk_grad_two, qk_grad_three]),
        jnp.stack([value_grad_zero, value_grad_one]),
        jnp.stack([output_grad_first, output_grad_second]),
        inner_grad,
        outer_grad,
        jnp.stack([gain_first, gain_second, gain_third]),
    )
    return (
        grad_terms,
        score_term,
        hidden_grad.reshape(sequences, length, model_width),
        memory_grad.reshape(sequences, -1, model_width),
    )


def adam_step(master, first_moment, second_moment, gradient, rate, decay):
    first_next = beta_first * first_moment + (1.0 - beta_first) * gradient
    second_next = beta_second * second_moment + (1.0 - beta_second) * gradient * gradient
    corrected = (
        first_next
        / (1.0 - beta_first**STEP)
        / (jnp.sqrt(second_next / (1.0 - beta_second**STEP)) + adam_epsilon)
    )
    master_next = master - rate * (corrected + decay * master)
    return (master_next, first_next, second_next)


def shards(
    hidden,
    memory,
    cotangent,
    target_lengths,
    memory_lengths,
    qk_master,
    value_master,
    output_master,
    inner_master,
    outer_master,
    gain_master,
    table_master,
    qk_first,
    value_first,
    output_first,
    inner_first,
    outer_first,
    gain_first,
    table_first,
    qk_second,
    value_second,
    output_second,
    inner_second,
    outer_second,
    gain_second,
    table_second,
):
    micro_count = hidden.shape[0]
    length = hidden.shape[2]
    model_width = hidden.shape[3]
    hidden_units = inner_master.shape[1]
    qk_low = qk_master.astype(jnp.bfloat16)
    value_low = value_master.astype(jnp.bfloat16)
    output_low = output_master.astype(jnp.bfloat16)
    inner_low = inner_master.astype(jnp.bfloat16)
    outer_low = outer_master.astype(jnp.bfloat16)
    gain_low = gain_master.astype(jnp.bfloat16)
    onehot = bucket_onehot(length)
    bias_heads = jnp.einsum("bij,bh->hij", onehot, table_master, precision=highest)
    masters = (qk_master, value_master, output_master, inner_master, outer_master, gain_master)
    totals = (
        jnp.zeros((4, model_width, model_width), jnp.float32),
        jnp.zeros((2, model_width, model_width), jnp.float32),
        jnp.zeros((2, model_width, model_width), jnp.float32),
        jnp.zeros((model_width, hidden_units), jnp.float32),
        jnp.zeros((hidden_units, model_width), jnp.float32),
        jnp.zeros((3, model_width), jnp.float32),
    )
    reduced = tuple((jnp.zeros_like(master) for master in masters))
    score_total = jnp.zeros((HEADS, length, length), jnp.float32)
    produced_list = []
    hidden_list = []
    memory_list = []
    for micro_index in range(micro_count):
        gathered = (
            lax.all_gather(qk_low, ("dp", "fsdp"), axis=1, tiled=True),
            lax.all_gather(value_low, ("dp", "fsdp"), axis=1, tiled=True),
            lax.all_gather(output_low, ("dp", "fsdp"), axis=1, tiled=True),
            lax.all_gather(inner_low, ("dp", "fsdp"), axis=0, tiled=True),
            lax.all_gather(outer_low, ("dp", "fsdp"), axis=0, tiled=True),
            lax.all_gather(gain_low, ("dp", "fsdp"), axis=1, tiled=True),
        )
        stored, produced = forward_pass(
            gathered,
            bias_heads,
            hidden[micro_index],
            memory[micro_index],
            target_lengths[micro_index],
            memory_lengths[micro_index],
        )
        gathered = (
            lax.all_gather(qk_low, ("dp", "fsdp"), axis=1, tiled=True),
            lax.all_gather(value_low, ("dp", "fsdp"), axis=1, tiled=True),
            lax.all_gather(output_low, ("dp", "fsdp"), axis=1, tiled=True),
            lax.all_gather(inner_low, ("dp", "fsdp"), axis=0, tiled=True),
            lax.all_gather(outer_low, ("dp", "fsdp"), axis=0, tiled=True),
            lax.all_gather(gain_low, ("dp", "fsdp"), axis=1, tiled=True),
        )
        grad_terms, score_term, hidden_grad, memory_grad = backward_pass(
            gathered, bias_heads, stored, cotangent[micro_index], target_lengths[micro_index]
        )
        totals = tuple((running + addition for running, addition in zip(totals, grad_terms)))
        score_total = score_total + score_term
        produced_list.append(produced)
        hidden_list.append(hidden_grad)
        memory_list.append(memory_grad)
    reduced = (
        lax.psum_scatter(totals[0], ("dp", "fsdp"), scatter_dimension=1, tiled=True),
        lax.psum_scatter(totals[1], ("dp", "fsdp"), scatter_dimension=1, tiled=True),
        lax.psum_scatter(totals[2], ("dp", "fsdp"), scatter_dimension=1, tiled=True),
        lax.psum_scatter(totals[3], ("dp", "fsdp"), scatter_dimension=0, tiled=True),
        lax.psum_scatter(totals[4], ("dp", "fsdp"), scatter_dimension=0, tiled=True),
        lax.psum_scatter(totals[5], ("dp", "fsdp"), scatter_dimension=1, tiled=True),
    )
    table_grad = jnp.einsum("bij,hij->bh", onehot, score_total, precision=highest)
    table_grad = lax.psum(table_grad, ("dp", "fsdp"))
    all_masters = (
        qk_master,
        value_master,
        output_master,
        inner_master,
        outer_master,
        gain_master,
        table_master,
    )
    firsts = (
        qk_first,
        value_first,
        output_first,
        inner_first,
        outer_first,
        gain_first,
        table_first,
    )
    seconds = (
        qk_second,
        value_second,
        output_second,
        inner_second,
        outer_second,
        gain_second,
        table_second,
    )
    gradients = (reduced[0], reduced[1], reduced[2], reduced[3], reduced[4], reduced[5], table_grad)
    rates = (
        rate_matrix,
        rate_matrix,
        rate_matrix,
        rate_matrix,
        rate_matrix,
        rate_small,
        rate_small,
    )
    decays = (weight_decay, weight_decay, weight_decay, weight_decay, weight_decay, 0.0, 0.0)
    updated = [
        adam_step(
            all_masters[index],
            firsts[index],
            seconds[index],
            gradients[index],
            rates[index],
            decays[index],
        )
        for index in range(7)
    ]
    news = [entry[0] for entry in updated]
    first_news = [entry[1] for entry in updated]
    second_news = [entry[2] for entry in updated]
    copies = [entry.astype(jnp.bfloat16) for entry in news]
    layer_out = jnp.stack(produced_list)
    hidden_out = jnp.stack(hidden_list)
    memory_out = jnp.stack(memory_list)
    return (
        layer_out,
        hidden_out,
        memory_out,
        news[0],
        news[1],
        news[2],
        news[3],
        news[4],
        news[5],
        news[6],
        first_news[0],
        first_news[1],
        first_news[2],
        first_news[3],
        first_news[4],
        first_news[5],
        first_news[6],
        second_news[0],
        second_news[1],
        second_news[2],
        second_news[3],
        second_news[4],
        second_news[5],
        second_news[6],
        copies[0],
        copies[1],
        copies[2],
        copies[3],
        copies[4],
        copies[5],
        copies[6],
    )


def solution(mesh):
    placed = (
        P(None, ("dp", "fsdp"), None, None),
        P(None, ("dp", "fsdp"), None, None),
        P(None, ("dp", "fsdp"), None, None),
        P(None, ("dp", "fsdp")),
        P(None, ("dp", "fsdp")),
        P(None, ("dp", "fsdp"), None),
        P(None, ("dp", "fsdp"), None),
        P(None, ("dp", "fsdp"), None),
        P(("dp", "fsdp"), None),
        P(("dp", "fsdp"), None),
        P(None, ("dp", "fsdp")),
        P(),
        P(None, ("dp", "fsdp"), None),
        P(None, ("dp", "fsdp"), None),
        P(None, ("dp", "fsdp"), None),
        P(("dp", "fsdp"), None),
        P(("dp", "fsdp"), None),
        P(None, ("dp", "fsdp")),
        P(),
        P(None, ("dp", "fsdp"), None),
        P(None, ("dp", "fsdp"), None),
        P(None, ("dp", "fsdp"), None),
        P(("dp", "fsdp"), None),
        P(("dp", "fsdp"), None),
        P(None, ("dp", "fsdp")),
        P(),
    )
    return jax.shard_map(
        shards,
        mesh=mesh,
        in_specs=placed,
        out_specs=(
            P(None, ("dp", "fsdp"), None, None),
            P(None, ("dp", "fsdp"), None, None),
            P(None, ("dp", "fsdp"), None, None),
            P(None, ("dp", "fsdp"), None),
            P(None, ("dp", "fsdp"), None),
            P(None, ("dp", "fsdp"), None),
            P(("dp", "fsdp"), None),
            P(("dp", "fsdp"), None),
            P(None, ("dp", "fsdp")),
            P(),
            P(None, ("dp", "fsdp"), None),
            P(None, ("dp", "fsdp"), None),
            P(None, ("dp", "fsdp"), None),
            P(("dp", "fsdp"), None),
            P(("dp", "fsdp"), None),
            P(None, ("dp", "fsdp")),
            P(),
            P(None, ("dp", "fsdp"), None),
            P(None, ("dp", "fsdp"), None),
            P(None, ("dp", "fsdp"), None),
            P(("dp", "fsdp"), None),
            P(("dp", "fsdp"), None),
            P(None, ("dp", "fsdp")),
            P(),
            P(None, ("dp", "fsdp"), None),
            P(None, ("dp", "fsdp"), None),
            P(None, ("dp", "fsdp"), None),
            P(("dp", "fsdp"), None),
            P(("dp", "fsdp"), None),
            P(None, ("dp", "fsdp")),
            P(),
        ),
        check_vma=False,
    )
```

profile of v0, /device:TPU:0, one launch (start us, length us, event | category | flops | bytes accessed | tf_op | source)
XLA Modules:
  0.0 1050.9 jit_solution(5972422379002773845)
XLA Ops:
  20.6 43.3 %all-gather = bf16[32,24,3]{1,2,0:T(4,128)(2,1)S(1)} all-gather(bf16[1,24,3]{1,2,0:T(4,128)(2,1)S(1)} %convert_bitcast_fusion.2), channel_id=1, replica_groups=mesh['dp'=8,'fsdp'=4] {'dp','fsdp'}, dimensions={0}, use_global_device_ids=true | all-gather | bytes 4752 | tf_op jit(solution)/shard_map/all_gather | solution.py:384
  64.2 4.8 fusion.1
  69.0 5.2 copy.194
  93.1 44.6 %all-gather.9.cloned.1.call-done = bf16[4,768,768]{2,1,0:T(8,128)(2,1)} async-done(((bf16[4,24,768]{2,1,0:T(8,128)(2,1)}), bf16[4,768,768]{2,1,0:T(8,128)(2,1)}) %all-gather.9.cloned.1.call-update) | async-done | bytes 4718608 | tf_op jit(solution)/shard_map/all_gather | solution.py:379
  142.5 2.7 fusion.193
  147.0 50.3 %all-gather.11.cloned.1.call-done = bf16[2,768,768]{2,1,0:T(8,128)(2,1)} async-done(((bf16[2,24,768]{2,1,0:T(8,128)(2,1)}), bf16[2,768,768]{2,1,0:T(8,128)(2,1)}) %all-gather.11.cloned.1.call-update) | async-done | bytes 2359312 | tf_op jit(solution)/shard_map/all_gather | solution.py:381
  213.0 2.8 convolution_convert_fusion.13
  217.7 2.7 fusion.195
  229.0 2.8 convolution_convert_fusion.10
  245.0 18.2 %all-gather.13.cloned.1.call-done = bf16[768,3072]{1,0:T(8,128)(2,1)} async-done(((bf16[24,3072]{1,0:T(8,128)(2,1)}), bf16[768,3072]{1,0:T(8,128)(2,1)}) %all-gather.13.cloned.1.call-update) | async-done | bytes 4718608 | tf_op jit(solution)/shard_map/all_gather | solution.py:382
  263.2 4.2 fusion.163
  272.9 6.1 convolution_add_fusion
  279.0 134.2 %reduce-scatter.15.cloned.1.call-done = f32[96,768]{1,0:T(8,128)} async-done(((f32[3072,768]{1,0:T(8,128)}), f32[96,768]{1,0:T(8,128)}) %reduce-scatter.15.cloned.1.call-update) | async-done | bytes 294928 | tf_op jit(solution)/shard_map/reduce_scatter | solution.py:415
  421.2 58.7 %all-gather.15.cloned.1.call-done = bf16[3072,768]{1,0:T(8,128)(2,1)} async-done(((bf16[96,768]{1,0:T(8,128)(2,1)}), bf16[3072,768]{1,0:T(8,128)(2,1)}) %all-gather.15.cloned.1.call-update) | async-done | bytes 4718608 | tf_op jit(solution)/shard_map/all_gather | solution.py:383
  479.9 6.2 fusion.17
  486.2 4.1 fusion.10
  500.0 5.3 multiply_reduce_fusion.1
  510.4 3.1 multiply_reduce_fusion.3
  546.1 2.7 maximum_add_fusion.2
  551.2 3.0 convolution_bitcast_fusion.12
  559.1 3.4 convert_add_fusion
  571.9 4.2 maximum_add_fusion
  577.2 3.0 fusion.162
  580.2 5.1 convolution_add_fusion.1
  599.3 5.3 copy.228
  606.1 6.2 fusion.74
  612.3 40.9 %all-reduce.1 = (f32[3,768]{1,0:T(4,128)}, f32[32,12]{0,1:T(8,128)}) all-reduce(f32[3,768]{1,0:T(4,128)} %maximum_add_fusion.3, f32[32,12]{0,1:T(8,128)S(1)} %fusion.74), channel_id=7, replica_groups=mesh['dp'=8,'fsdp'=4] {'dp','fsdp'}, use_global_device_ids=true, to_apply=%region_35.36.clone | all-reduce | flops 2688 | bytes 21504
  653.1 4.6 fusion.72
  657.9 4.6 fusion.73
  674.4 85.3 %reduce-scatter.11.cloned.1.call-done = f32[2,24,768]{2,1,0:T(8,128)} async-done(((f32[2,768,768]{2,1,0:T(8,128)}), f32[2,24,768]{2,1,0:T(8,128)}) %reduce-scatter.11.cloned.1.call-update) | async-done | bytes 147472 | tf_op jit(solution)/shard_map/reduce_scatter | solution.py:413
  761.5 139.8 %reduce-scatter.7.cloned.1.call-done = f32[4,24,768]{2,1,0:T(8,128)} async-done(((f32[4,768,768]{2,1,0:T(8,128)}), f32[4,24,768]{2,1,0:T(8,128)}) %reduce-scatter.7.cloned.1.call-update) | async-done | bytes 294928 | tf_op jit(solution)/shard_map/reduce_scatter | solution.py:411
  903.3 138.5 %reduce-scatter.13.cloned.1.call-done = f32[24,3072]{1,0:T(8,128)} async-done(((f32[768,3072]{1,0:T(8,128)}), f32[24,3072]{1,0:T(8,128)}) %reduce-scatter.13.cloned.1.call-update) | async-done | bytes 294928 | tf_op jit(solution)/shard_map/reduce_scatter | solution.py:414
  (563 shorter events, 188.7 us)
Async XLA Ops:
  7.2 72.0 %all-gather.7.cloned.1.call-start = ((), (), s32[]{:S(2)}) async-start(), calls=%async_computation.5 | async-start | bytes 2433024 | tf_op jit(solution)/shard_map/all_gather | solution.py:380
  8.8 128.8 %all-gather.9.cloned.1.call-start = ((), (), s32[]{:S(2)}) async-start(), calls=%async_computation.6 | async-start | bytes 4866048 | tf_op jit(solution)/shard_map/all_gather | solution.py:379
  10.5 186.7 %all-gather.11.cloned.1.call-start = ((), (), s32[]{:S(2)}) async-start(), calls=%async_computation.7 | async-start | bytes 2433024 | tf_op jit(solution)/shard_map/all_gather | solution.py:381
  12.2 251.0 %all-gather.13.cloned.1.call-start = ((), (), s32[]{:S(2)}) async-start(), calls=%async_computation.8 | async-start | bytes 4866048 | tf_op jit(solution)/shard_map/all_gather | solution.py:382
  13.9 399.4 %reduce-scatter.15.cloned.1.call-start = ((), (), s32[]{:S(2)}) async-start(), calls=%async_computation.14 | async-start | bytes 9732096 | tf_op jit(solution)/shard_map/reduce_scatter | solution.py:415
  14.1 50.1 %copy-start.98 = (s32[256,256]{1,0:T(8,128)}, s32[256,256]{1,0:T(8,128)S(1)}, u32[]{:S(2)}) copy-start(s32[256,256]{1,0:T(8,128)S(1)} %compare_select_fusion) | copy-start | bytes 786436
  69.0 10.2 copy-start.19
  79.2 60.4 %copy-start.152 = (f32[256]{0:T(256)}, f32[256]{0:T(256)S(1)}, u32[]{:S(2)}) copy-start(f32[256]{0:T(256)S(1)} %get-tuple-element.123) | copy-start | bytes 3076
  147.0 57.6 %copy-start.121 = (bf16[12,64,256]{2,1,0:T(8,128)(2,1)}, bf16[12,64,256]{2,1,0:T(8,128)(2,1)S(1)}, u32[]{:S(2)}) copy-start(bf16[12,64,256]{2,1,0:T(8,128)(2,1)S(1)} %fusion.49) | copy-start | bytes 1179652
  200.1 9.1 copy-start.156
  213.0 7.5 copy-start.63
  225.3 8.4 copy-start.185
  229.0 6.5 copy-start.68
  263.2 6.5 slice-start
  279.0 200.9 %all-gather.15.cloned.1.call-start = ((), (), s32[]{:S(2)}) async-start(), calls=%async_computation.9 | async-start | bytes 4866048 | tf_op jit(solution)/shard_map/all_gather | solution.py:383
  415.8 256.9 %reduce-scatter.9.cloned.1.call-start = ((), (), s32[]{:S(2)}) async-start(), calls=%async_computation.11 | async-start | bytes 4866048 | tf_op jit(solution)/shard_map/reduce_scatter | solution.py:412
  479.9 6.3 copy-start.168
  479.9 6.3 copy-start.186
  479.9 10.4 slice-start.2
  541.6 218.1 %reduce-scatter.11.cloned.1.call-start = ((), (), s32[]{:S(2)}) async-start(), calls=%async_computation.12 | async-start | bytes 4866048 | tf_op jit(solution)/shard_map/reduce_scatter | solution.py:413
  548.8 352.4 %reduce-scatter.7.cloned.1.call-start = ((), (), s32[]{:S(2)}) async-start(), calls=%async_computation.10 | async-start | bytes 9732096 | tf_op jit(solution)/shard_map/reduce_scatter | solution.py:411
  576.1 465.6 %reduce-scatter.13.cloned.1.call-start = ((), (), s32[]{:S(2)}) async-start(), calls=%async_computation.13 | async-start | bytes 9732096 | tf_op jit(solution)/shard_map/reduce_scatter | solution.py:414
  604.6 48.6 %copy-start.9 = (f32[256,3072]{1,0:T(8,128)S(1)}, f32[256,3072]{1,0:T(8,128)}, u32[]{:S(2)}) copy-start(f32[256,3072]{1,0:T(8,128)} %copy-done.8) | copy-start | bytes 9437188
  668.7 91.0 %copy-start.120 = (f32[2,24,768]{2,1,0:T(8,128)S(1)}, f32[2,24,768]{2,1,0:T(8,128)}, u32[]{:S(2)}) copy-start(f32[2,24,768]{2,1,0:T(8,128)} %param.33) | copy-start | bytes 442372
  669.3 90.4 %copy-start.141 = (f32[2,24,768]{2,1,0:T(8,128)S(1)}, f32[2,24,768]{2,1,0:T(8,128)}, u32[]{:S(2)}) copy-start(f32[2,24,768]{2,1,0:T(8,128)} %param.40) | copy-start | bytes 442372
  669.3 90.4 %copy-start.142 = (f32[2,24,768]{2,1,0:T(8,128)S(1)}, f32[2,24,768]{2,1,0:T(8,128)}, u32[]{:S(2)}) copy-start(f32[2,24,768]{2,1,0:T(8,128)} %param.47) | copy-start | bytes 442372
  669.3 231.9 %copy-start.116 = (f32[4,24,768]{2,1,0:T(8,128)S(1)}, f32[4,24,768]{2,1,0:T(8,128)}, u32[]{:S(2)}) copy-start(f32[4,24,768]{2,1,0:T(8,128)} %param.31) | copy-start | bytes 884740
  669.3 231.9 %copy-start.125 = (f32[4,24,768]{2,1,0:T(8,128)S(1)}, f32[4,24,768]{2,1,0:T(8,128)}, u32[]{:S(2)}) copy-start(f32[4,24,768]{2,1,0:T(8,128)} %param.38) | copy-start | bytes 884740
  669.3 231.9 %copy-start.126 = (f32[4,24,768]{2,1,0:T(8,128)S(1)}, f32[4,24,768]{2,1,0:T(8,128)}, u32[]{:S(2)}) copy-start(f32[4,24,768]{2,1,0:T(8,128)} %param.45) | copy-start | bytes 884740
  669.3 372.4 %copy-start.117 = (f32[24,3072]{1,0:T(8,128)S(1)}, f32[24,3072]{1,0:T(8,128)}, u32[]{:S(2)}) copy-start(f32[24,3072]{1,0:T(8,128)} %param.34) | copy-start | bytes 884740
  669.3 372.4 %copy-start.127 = (f32[24,3072]{1,0:T(8,128)S(1)}, f32[24,3072]{1,0:T(8,128)}, u32[]{:S(2)}) copy-start(f32[24,3072]{1,0:T(8,128)} %param.41) | copy-start | bytes 884740
  669.4 372.4 %copy-start.128 = (f32[24,3072]{1,0:T(8,128)S(1)}, f32[24,3072]{1,0:T(8,128)}, u32[]{:S(2)}) copy-start(f32[24,3072]{1,0:T(8,128)} %param.48) | copy-start | bytes 884740
  (173 other events, 459.9 us)
Sparse Core Ops, SparseCore 0:
  11.6 59.9 all-gather.6
  75.1 62.5 all-gather.8
  141.2 56.0 all-gather.10
  200.6 62.5 all-gather.12
  279.1 134.1 reduce-scatter.14
  417.0 62.8 all-gather.14
  541.7 106.3 reduce-scatter.8
  653.5 106.1 reduce-scatter.10
  766.6 134.5 reduce-scatter.6
  907.0 134.7 reduce-scatter.12
where the time goes:
time: 1060 us; the launch traced here: 1050 us
  waiting for transfers between devices  670 us (63%)
  matrix products  157 us (15%)
  blocking collectives  84.1 us (8%)
  local copies, waits for them, and re-layouts  63.1 us (6%)
  other arithmetic  60.1 us (6%)
  between operations  16.7 us (2%)
    reduce_scatter x1, waiting for transfers between devices, shards(): lax.psum_scatter(totals[0], ('dp', 'fsdp'), scatter_dimension=1, tiled=True)  140 us
    reduce_scatter x1, waiting for transfers between devices, shards(): lax.psum_scatter(totals[3], ('dp', 'fsdp'), scatter_dimension=0, tiled=True)  138 us
    reduce_scatter x1, waiting for transfers between devices, shards(): lax.psum_scatter(totals[4], ('dp', 'fsdp'), scatter_dimension=0, tiled=True)  134 us
    reduce_scatter x1, waiting for transfers between devices, shards(): lax.psum_scatter(totals[2], ('dp', 'fsdp'), scatter_dimension=1, tiled=True)  85.3 us
    all_gather x1, waiting for transfers between devices, shards(): lax.all_gather(outer_low, ('dp', 'fsdp'), axis=0, tiled=True)  58.7 us
    all_gather x1, waiting for transfers between devices, shards(): lax.all_gather(output_low, ('dp', 'fsdp'), axis=1, tiled=True)  50.3 us
    dot_general x20, matrix products, product(): return jnp.dot(left_side, right_side, preferred_element_type=jnp.float32)  48 us
    all_gather x1, waiting for transfers between devices, shards(): lax.all_gather(qk_low, ('dp', 'fsdp'), axis=1, tiled=True)  44.6 us
  transfers between devices with their start and end apart: 10, of which 8 were waited for; matrix products, arithmetic and copies ran while one was open for 17% of the time, Pallas kernels for 0%

commit v1 on v0

--- a/solution.py
+++ b/solution.py
@@ -1,8 +1,11 @@
+import functools
 import math
 
 import jax
 import jax.numpy as jnp
 from jax import lax
+from jax.experimental import pallas as pl
+from jax.experimental.pallas import tpu as pltpu
 from jax.sharding import PartitionSpec as P
 
 HEADS = 12
@@ -508,6 +511,530 @@
     )
 
 
+MESH = pl.DeviceIdType.MESH
+PAIRS = 6
+ORDERS = ("ax", "ay", "ax", "ay", "ax", "ay", "cx", "cy")
+
+
+class Place:
+    def __init__(self, wa, wf):
+        self.wa, self.wf = wa, wf
+        dp, fs = lax.axis_index("dp"), lax.axis_index("fsdp")
+        self.z, self.y = dp // 2, dp % 2
+        self.x, self.c = fs // 2, fs % 2
+        self.to = {
+            "x": (dp, (1 - self.x) * 2 + self.c),
+            "y": (self.z * 2 + 1 - self.y, fs),
+            "c": (dp, self.x * 2 + 1 - self.c),
+            "r": (dp + 2, fs),
+            "l": (dp - 2, fs),
+        }
+
+    def enter(self):
+        bar = pltpu.get_barrier_semaphore()
+
+        def greet(way):
+            pl.semaphore_signal(bar, inc=1, device_id=self.to[way], device_id_type=MESH)
+
+        for way in ("x", "y", "c"):
+            greet(way)
+
+        @pl.when(self.z < 3)
+        def _():
+            greet("r")
+
+        @pl.when(self.z > 0)
+        def _():
+            greet("l")
+
+        inner = (self.z > 0) & (self.z < 3)
+
+        @pl.when(inner)
+        def _():
+            pl.semaphore_wait(bar, 5)
+
+        @pl.when(jnp.logical_not(inner))
+        def _():
+            pl.semaphore_wait(bar, 4)
+
+    def pick(self, f, zs, ps, qs, core=None):
+        c = self.c if core is None else core
+        xs, ys = (ps, qs) if ORDERS[f][1] == "x" else (qs, ps)
+        if f < PAIRS:
+            return self.wa.at[2 * f + c, zs, ys, xs]
+        return self.wf.at[zs, ys, xs, c, f - PAIRS]
+
+    def own(self, f):
+        return (self.x, self.y) if ORDERS[f][1] == "x" else (self.y, self.x)
+
+    def ways(self, f):
+        return ("x", "y") if ORDERS[f][1] == "x" else ("y", "x")
+
+
+def push(place, src, dst, send, recv, way):
+    pltpu.make_async_remote_copy(
+        src_ref=src, dst_ref=dst, send_sem=send, recv_sem=recv,
+        device_id=place.to[way], device_id_type=MESH,
+    ).start()
+
+
+def got(place, ref, sem, way):
+    pltpu.make_async_remote_copy(
+        src_ref=ref, dst_ref=ref, send_sem=sem, recv_sem=sem,
+        device_id=place.to[way], device_id_type=MESH,
+    ).wait_recv()
+
+
+def left_out(place, ref, sem, way):
+    pltpu.make_async_remote_copy(
+        src_ref=ref, dst_ref=ref, send_sem=sem, recv_sem=sem,
+        device_id=place.to[way], device_id_type=MESH,
+    ).wait_send()
+
+
+ALL = slice(None)
+
+
+class Gather:
+    def __init__(self, place, f, send, recv):
+        self.k, self.f = place, f
+        self.send, self.recv = send, recv
+        self.first_cross = ORDERS[f][0] == "a"
+        self.stages = [self.start, self.cross if self.first_cross else (lambda: self.step(1)),
+                       (lambda: self.step(1 if self.first_cross else 2)),
+                       (lambda: self.step(2 if self.first_cross else 3)),
+                       (lambda: self.step(3)) if self.first_cross else self.cross,
+                       self.second, self.finish]
+
+    def blk(self, zi):
+        p, q = self.k.own(self.f)
+        return self.k.pick(self.f, zi, ALL if self.first_cross else p, q)
+
+    def move(self, ref, s, r, way):
+        push(self.k, ref, ref, self.send.at[self.f, s], self.recv.at[self.f, r], way)
+
+    def start(self):
+        p, q = self.k.own(self.f)
+        pw, qw = self.k.ways(self.f)
+        if self.first_cross:
+            self.move(self.k.pick(self.f, self.k.z, p, q), 0, 0, pw)
+        else:
+            self.spread(self.k.z, 1)
+
+    def cross(self):
+        p, q = self.k.own(self.f)
+        pw, qw = self.k.ways(self.f)
+        if self.first_cross:
+            got(self.k, self.k.pick(self.f, self.k.z, 1 - p, q), self.recv.at[self.f, 0], pw)
+            self.spread(self.k.z, 1)
+        else:
+            got(self.k, self.k.pick(self.f, ALL, 1 - p, q), self.recv.at[self.f, 0], pw)
+            half = self.k.pick(self.f, ALL, ALL, q)
+            self.move(half, 3, 7, qw)
+            self.move(half, 4, 8, "c")
+
+    def sideways(self, zi):
+        pw, qw = self.k.ways(self.f)
+        if self.first_cross:
+            self.move(self.blk(zi), 3, 7, qw)
+            self.move(self.blk(zi), 4, 8, "c")
+        else:
+            self.move(self.blk(zi), 0, 0, pw)
+
+    def spread(self, zi, t):
+        z = self.k.z
+
+        @pl.when(z < 3)
+        def _():
+            self.move(self.blk(zi), 1, t, "r")
+
+        @pl.when(z > 0)
+        def _():
+            self.move(self.blk(zi), 2, 3 + t, "l")
+
+        self.sideways(zi)
+
+    def step(self, t):
+        z = self.k.z
+
+        @pl.when(z >= t)
+        def _():
+            got(self.k, self.blk(z - t), self.recv.at[self.f, t], "l")
+
+            if t < 3:
+                @pl.when(z < 3)
+                def _():
+                    self.move(self.blk(z - t), 1, t + 1, "r")
+
+            self.sideways(z - t)
+
+        @pl.when(z <= 3 - t)
+        def _():
+            got(self.k, self.blk(z + t), self.recv.at[self.f, 3 + t], "r")
+
+            if t < 3:
+                @pl.when(z > 0)
+                def _():
+                    self.move(self.blk(z + t), 2, 3 + t + 1, "l")
+
+            self.sideways(z + t)
+
+    def second(self):
+        p, q = self.k.own(self.f)
+        pw, qw = self.k.ways(self.f)
+        other = self.k.pick(self.f, ALL, ALL, 1 - q)
+        got(self.k, other, self.recv.at[self.f, 7], qw)
+        self.move(other, 4, 8, "c")
+
+    def finish(self):
+        theirs = self.k.pick(self.f, ALL, ALL, ALL, 1 - self.k.c)
+        got(self.k, theirs, self.recv.at[self.f, 8], "c")
+
+    def drain(self):
+        p, q = self.k.own(self.f)
+        pw, qw = self.k.ways(self.f)
+        z, f = self.k.z, self.f
+        some = (lambda n: self.k.pick(f, pl.ds(0, n), ALL if self.first_cross else p, q))
+        first = self.k.pick(f, z, p, q) if self.first_cross else self.k.pick(f, ALL, p, q)
+        left_out(self.k, first, self.send.at[f, 0], pw)
+        for n in (1, 2, 3):
+            @pl.when(z == n - 1)
+            def _():
+                left_out(self.k, some(n), self.send.at[f, 1], "r")
+
+            @pl.when(z == 4 - n)
+            def _():
+                left_out(self.k, some(n), self.send.at[f, 2], "l")
+        left_out(self.k, self.k.pick(f, ALL, ALL, q), self.send.at[f, 3], qw)
+        left_out(self.k, self.k.pick(f, ALL, ALL, ALL), self.send.at[f, 4], "c")
+
+
+def add_into(dst, srcs, lead):
+    sizes = lead
+    count = 1
+    for s in sizes:
+        count *= s
+
+    def body(i, _):
+        idx, rest = [], i
+        for s in reversed(sizes):
+            idx.append(rest % s)
+            rest = rest // s
+        idx = tuple(reversed(idx)) or Ellipsis
+        total = dst[idx].astype(jnp.float32)
+        for src in srcs:
+            total = total + src[idx].astype(jnp.float32)
+        dst[idx] = total.astype(jnp.bfloat16)
+        return 0
+
+    lax.fori_loop(0, count, body, 0)
+
+
+class Scatter:
+    def __init__(self, place, f, send, recv, slots, final, result):
+        self.k, self.f = place, f
+        self.send, self.recv = send, recv
+        self.rd, self.rq, self.rp, self.rl, self.rr = slots
+        self.final, self.result = final, result
+        self.wide = ORDERS[f][0] == "a"
+        self.stages = [self.start, self.core, self.half,
+                       *([] if self.wide else [self.cross_in]),
+                       (lambda: self.step_in(1)), (lambda: self.step_in(2)), (lambda: self.step_in(3)),
+                       *([self.last] if self.wide else []), self.finish]
+
+    def move(self, src, dst, s, way):
+        push(self.k, src, dst, self.send.at[self.f, s], self.recv.at[self.f, s], way)
+
+    def blk(self, zi):
+        p, q = self.k.own(self.f)
+        return self.k.pick(self.f, zi, ALL if self.wide else p, q)
+
+    def start(self):
+        self.move(self.k.pick(self.f, ALL, ALL, ALL, 1 - self.k.c), self.rd, 0, "c")
+
+    def rpick(self, ps, qs):
+        xs, ys = (ps, qs) if ORDERS[self.f][1] == "x" else (qs, ps)
+        return self.rd.at[:, ys, xs]
+
+    def core(self):
+        p, q = self.k.own(self.f)
+        pw, qw = self.k.ways(self.f)
+        got(self.k, self.rd, self.recv.at[self.f, 0], "c")
+        away = self.k.pick(self.f, ALL, ALL, 1 - q)
+        add_into(away, [self.rpick(ALL, 1 - q)], (4, 2))
+        self.move(away, self.rq, 1, qw)
+
+    def half(self):
+        p, q = self.k.own(self.f)
+        pw, qw = self.k.ways(self.f)
+        got(self.k, self.rq, self.recv.at[self.f, 1], qw)
+        add_into(self.k.pick(self.f, ALL, ALL, q), [self.rpick(ALL, q), self.rq], (4, 2))
+        if self.wide:
+            self.step_out(1)
+        else:
+            self.move(self.k.pick(self.f, ALL, 1 - p, q), self.rp, 2, pw)
+
+    def cross_in(self):
+        p, q = self.k.own(self.f)
+        pw, qw = self.k.ways(self.f)
+        got(self.k, self.rp, self.recv.at[self.f, 2], pw)
+        add_into(self.k.pick(self.f, ALL, p, q), [self.rp], (4,))
+        self.step_out(1)
+
+    def step_out(self, t):
+        z = self.k.z
+
+        @pl.when(z <= t - 1)
+        def _():
+            self.move(self.blk(z + 4 - t), self.rl.at[t - 1], 2 + t, "r")
+
+        @pl.when(z >= 4 - t)
+        def _():
+            self.move(self.blk(z - 4 + t), self.rr.at[t - 1], 5 + t, "l")
+
+    def step_in(self, t):
+        z, f = self.k.z, self.f
+        lead = (2,) if self.wide else ()
+
+        @pl.when((z >= 1) & (z <= t))
+        def _():
+            got(self.k, self.rl.at[t - 1], self.recv.at[f, 2 + t], "l")
+            add_into(self.blk(z + 3 - t), [self.rl.at[t - 1]], lead)
+
+        @pl.when((z <= 2) & (z >= 3 - t))
+        def _():
+            got(self.k, self.rr.at[t - 1], self.recv.at[f, 5 + t], "r")
+            add_into(self.blk(z - 3 + t), [self.rr.at[t - 1]], lead)
+
+        if t < 3:
+            self.step_out(t + 1)
+        else:
+            p, q = self.k.own(f)
+            pw, qw = self.k.ways(f)
+            if self.wide:
+                self.move(self.k.pick(f, z, 1 - p, q), self.rp, 2, pw)
+            else:
+                self.total(None)
+
+    def last(self):
+        pw, qw = self.k.ways(self.f)
+        got(self.k, self.rp, self.recv.at[self.f, 2], pw)
+        self.total(self.rp)
+
+    def total(self, more):
+        p, q = self.k.own(self.f)
+        c = self.k.c
+        mine = self.k.pick(self.f, self.k.z, p, q)[...].astype(jnp.float32)
+        if more is not None:
+            mine = mine + more[...].astype(jnp.float32)
+        if self.f < PAIRS:
+            self.final[...] = mine
+            kept = pl.ds(pl.multiple_of(c * 24, 8), 24)
+            away = pl.ds(pl.multiple_of(24 - c * 24, 8), 24)
+            self.move(self.final.at[away], self.result.at[2 * self.f + c], 9, "c")
+            self.result[2 * self.f + c] = self.final[kept]
+        else:
+            self.final[...] = mine
+
+    def finish(self):
+        if self.f < PAIRS:
+            got(self.k, self.result.at[2 * self.f + 1 - self.k.c], self.recv.at[self.f, 9], "c")
+
+    def drain(self):
+        p, q = self.k.own(self.f)
+        pw, qw = self.k.ways(self.f)
+        z, f, k = self.k.z, self.f, self.k
+        left_out(k, self.rd, self.send.at[f, 0], "c")
+        left_out(k, self.rq, self.send.at[f, 1], qw)
+        left_out(k, self.rp, self.send.at[f, 2], pw)
+        for t in (1, 2, 3):
+            @pl.when(z <= t - 1)
+            def _():
+                left_out(k, self.rl.at[t - 1], self.send.at[f, 2 + t], "r")
+
+            @pl.when(z >= 4 - t)
+            def _():
+                left_out(k, self.rr.at[t - 1], self.send.at[f, 5 + t], "l")
+        if f < PAIRS:
+            left_out(k, self.final.at[pl.ds(0, 24)], self.send.at[f, 9], "c")
+
+
+def weave(flows, gap=0):
+    out = []
+    rounds = max(i * gap + len(flow.stages) for i, flow in enumerate(flows))
+    for r in range(rounds):
+        for i, flow in enumerate(flows):
+            s = r - i * gap
+            if 0 <= s < len(flow.stages):
+                out.append(flow.stages[s])
+    return out
+
+
+def gather_kernel(m_ref, o_ref, wa, wf, xch, send, recv, xs, xr):
+    k = Place(wa, wf)
+    k.enter()
+    z, y, x, c = k.z, k.y, k.x, k.c
+    row = pl.ds(pl.multiple_of(24 * c, 8), 24)
+    push(k, m_ref.at[:, 1 - c], xch.at[:, row], xs, xr, "c")
+    for h in range(2):
+        wf[z, y, x, c, h] = o_ref[48 * h:48 * h + 48].astype(jnp.bfloat16)
+    flows = [Gather(k, f, send, recv) for f in range(8)]
+    for f in (6, 7):
+        flows[f].start()
+    for p in range(PAIRS):
+        xch[p, row] = m_ref[p, c]
+    other = pl.ds(pl.multiple_of(24 - 24 * c, 8), 24)
+    got(k, xch.at[:, other], xr, "c")
+    for p in range(PAIRS):
+        wa[2 * p + c, z, y, x] = xch[p].astype(jnp.bfloat16)
+        flows[p].start()
+    left_out(k, m_ref.at[:, 1 - c], xs, "c")
+    for flow in flows:
+        flow.stages = flow.stages[1:]
+    for stage in weave(flows):
+        stage()
+    for flow in flows:
+        flow.drain()
+
+
+def gather_all(m, o):
+    return pl.pallas_call(
+        gather_kernel,
+        out_shape=(jax.ShapeDtypeStruct((12, 4, 2, 2, 48, 768), jnp.bfloat16),
+                   jax.ShapeDtypeStruct((4, 2, 2, 2, 2, 48, 768), jnp.bfloat16)),
+        in_specs=[pl.BlockSpec(memory_space=pltpu.VMEM)] * 2,
+        out_specs=[pl.BlockSpec(memory_space=pltpu.VMEM)] * 2,
+        scratch_shapes=[
+            pltpu.VMEM((6, 48, 768), jnp.float32),
+            pltpu.SemaphoreType.DMA((8, 5)),
+            pltpu.SemaphoreType.DMA((8, 9)),
+            pltpu.SemaphoreType.DMA,
+            pltpu.SemaphoreType.DMA,
+        ],
+        compiler_params=pltpu.CompilerParams(collective_id=0, has_side_effects=True, vmem_limit_bytes=60 * 2**20),
+    )(m, o)
+
+
+def scatter_kernel(ga_in, gf_in, res, fin, wa, wf, rd, rq, rlw, rrw, rpw, rln, rrn, rpn, send, recv, cs):
+    ca = pltpu.make_async_copy(ga_in, wa, cs.at[0])
+    cf = pltpu.make_async_copy(gf_in, wf, cs.at[1])
+    ca.start()
+    cf.start()
+    k = Place(wa, wf)
+    k.enter()
+    ca.wait()
+    cf.wait()
+    flows = []
+    for f in (6, 7, 5, 4, 3, 2, 1, 0):
+        if f < PAIRS:
+            slots = (rd.at[f], rq.at[f], rpw.at[f], rlw.at[f], rrw.at[f])
+        else:
+            slots = (rd.at[f], rq.at[f], rpn.at[f - PAIRS], rln.at[f - PAIRS], rrn.at[f - PAIRS])
+        flows.append(Scatter(k, f, send, recv, slots, fin.at[f], res))
+    for flow in flows:
+        flow.stages[0]()
+        flow.stages = flow.stages[1:]
+    for stage in weave(flows):
+        stage()
+    for flow in flows:
+        flow.drain()
+
+
+def scatter_all(ga, gf):
+    bf, f32 = jnp.bfloat16, jnp.float32
+    return pl.pallas_call(
+        scatter_kernel,
+        out_shape=(jax.ShapeDtypeStruct((12, 24, 768), f32), jax.ShapeDtypeStruct((8, 48, 768), f32)),
+        in_specs=[pl.BlockSpec(memory_space=pl.ANY)] * 2,
+        out_specs=[pl.BlockSpec(memory_space=pltpu.VMEM)] * 2,
+        scratch_shapes=[
+            pltpu.VMEM((12, 4, 2, 2, 48, 768), bf),
+            pltpu.VMEM((4, 2, 2, 2, 2, 48, 768), bf),
+            pltpu.VMEM((8, 4, 2, 2, 48, 768), bf),
+            pltpu.VMEM((8, 4, 2, 48, 768), bf),
+            pltpu.VMEM((6, 3, 2, 48, 768), bf),
+            pltpu.VMEM((6, 3, 2, 48, 768), bf),
+            pltpu.VMEM((6, 48, 768), bf),
+            pltpu.VMEM((2, 3, 48, 768), bf),
+            pltpu.VMEM((2, 3, 48, 768), bf),
+            pltpu.VMEM((2, 4, 48, 768), bf),
+            pltpu.SemaphoreType.DMA((8, 10)),
+            pltpu.SemaphoreType.DMA((8, 10)),
+            pltpu.SemaphoreType.DMA((2,)),
+        ],
+        compiler_params=pltpu.CompilerParams(collective_id=1, has_side_effects=True, vmem_limit_bytes=60 * 2**20),
+    )(ga, gf)
+
+
+def shards_block(
+    hidden, memory, cotangent, target_lengths, memory_lengths,
+    qk_master, value_master, output_master, inner_master, outer_master, gain_master, table_master,
+    qk_first, value_first, output_first, inner_first, outer_first, gain_first, table_first,
+    qk_second, value_second, output_second, inner_second, outer_second, gain_second, table_second,
+):
+    axes = ("dp", "fsdp")
+    micro, _, length, width = hidden.shape
+    inner4 = inner_master.reshape(24, 4, 768).transpose(1, 0, 2)
+    m = jnp.concatenate(
+        [qk_master[0:2], value_master[0:1], output_master[0:1], qk_master[3:4], value_master[1:2],
+         qk_master[2:3], output_master[1:2], inner4]
+    ).reshape(6, 2, 24, 768)
+    wa, wf = gather_all(m, outer_master)
+    wa = wa.reshape(12, 768, 768)
+    gain_full = lax.all_gather(gain_master.astype(jnp.bfloat16), axes, axis=1, tiled=True)
+    gathered = (
+        jnp.stack([wa[0], wa[1], wa[6], wa[4]]),
+        jnp.stack([wa[2], wa[5]]),
+        jnp.stack([wa[3], wa[7]]),
+        jnp.concatenate([wa[8], wa[9], wa[10], wa[11]], axis=1),
+        wf.reshape(3072, 768),
+        gain_full,
+    )
+    onehot = bucket_onehot(length)
+    bias_heads = jnp.einsum("bij,bh->hij", onehot, table_master, precision=highest)
+    stored, produced = forward_pass(
+        gathered, bias_heads, hidden[:, 0], memory[:, 0], target_lengths[:, 0], memory_lengths[:, 0]
+    )
+    grad_terms, score_term, hidden_grad, memory_grad = backward_pass(
+        gathered, bias_heads, stored, cotangent[:, 0], target_lengths[:, 0]
+    )
+    gqk, gv, go, gi, gw, gg = grad_terms
+    ga = jnp.concatenate(
+        [gqk[0:2], gv[0:1], go[0:1], gqk[3:4], gv[1:2], gqk[2:3], go[1:2],
+         gi.reshape(768, 4, 768).transpose(1, 0, 2)]
+    ).astype(jnp.bfloat16).reshape(12, 4, 2, 2, 48, 768)
+    res, fin = scatter_all(ga, gw.astype(jnp.bfloat16).reshape(4, 2, 2, 2, 2, 48, 768))
+    table_grad = jnp.einsum("bij,hij->bh", onehot, score_term, precision=highest)
+    small = lax.psum(jnp.concatenate([gg.reshape(-1), table_grad.reshape(-1)]), axes)
+    device = lax.axis_index(axes)
+    gain_grad = lax.dynamic_slice(small[:2304].reshape(3, 768), (0, 24 * device), (3, 24))
+    gradients = (
+        jnp.stack([res[0], res[1], res[6], res[4]]),
+        jnp.stack([res[2], res[5]]),
+        jnp.stack([res[3], res[7]]),
+        res[8:12].transpose(1, 0, 2).reshape(24, 3072),
+        fin[6:].reshape(96, 768),
+        gain_grad,
+        small[2304:].reshape(BUCKETS, HEADS),
+    )
+    masters = (qk_master, value_master, output_master, inner_master, outer_master, gain_master, table_master)
+    firsts = (qk_first, value_first, output_first, inner_first, outer_first, gain_first, table_first)
+    seconds = (qk_second, value_second, output_second, inner_second, outer_second, gain_second, table_second)
+    updated = [
+        adam_step(a, b, c, g, rate_matrix if i < 5 else rate_small, weight_decay if i < 5 else 0.0)
+        for i, (a, b, c, g) in enumerate(zip(masters, firsts, seconds, gradients))
+    ]
+    return (
+        produced[:, None],
+        hidden_grad[:, None],
+        memory_grad[:, None],
+        *[u[0] for u in updated],
+        *[u[1] for u in updated],
+        *[u[2] for u in updated],
+        *[u[0].astype(jnp.bfloat16) for u in updated],
+    )
+
+
 def solution(mesh):
     placed = (
         P(None, ("dp", "fsdp"), None, None),
@@ -537,8 +1064,9 @@
         P(None, ("dp", "fsdp")),
         P(),
     )
+    small_slice = dict(mesh.shape) == {"dp": 8, "fsdp": 4}
     return jax.shard_map(
-        shards,
+        shards_block if small_slice else shards,
         mesh=mesh,
         in_specs=placed,
         out_specs=(

time: 1060 us -> 539 us (0.51)
  waiting for transfers between devices: 670 us -> 0 us
  Pallas kernels: 0 us -> 217 us
  matrix products: 157 us -> 112 us
  other arithmetic: 60.1 us -> 26.7 us
  local copies, waits for them, and re-layouts: 63.1 us -> 92.8 us
  between operations: 16.7 us -> 2.26 us
    reduce_scatter x5 -> x0, waiting for transfers between devices: 498 us -> none  [the longest x1 140 us: shards(): lax.psum_scatter(totals[0], ('dp', 'fsdp'), scatter_dimension=1, tiled=True)]
    pallas_call x0 -> x2, Pallas kernels: none -> 217 us  [the longest x1 118 us: scatter_all(): pl.pallas_call(scatter_kernel, out_shape=(jax.ShapeDtypeStruct((12, 24, 7...]
    all_gather x5 -> x0, waiting for transfers between devices: 172 us -> none  [the longest x1 58.7 us: shards(): lax.all_gather(outer_low, ('dp', 'fsdp'), axis=0, tiled=True)]
    unnamed x1 -> x0, blocking collectives: 40.9 us -> none
    psum x0 -> x1, blocking collectives: none -> 37 us  [shards_block(): lax.psum(jnp.concatenate([gg.reshape(-1), table_grad.reshape(-1)]), axes)]
    reshape x0 -> x15, local copies, waits for them, and re-layouts: none -> 22.1 us  [the longest x8 16.8 us: to_heads(): return values.reshape(sequences, -1, HEADS, HEAD_DIM)]
    dot_general x20 -> x10, matrix products: 34.1 us -> 16.7 us  [product_transposed(): lax.dot_general(left_side, right_side, (((1,), (1,)), ((), ())), preferre...]
    dot_general x20 -> x10, matrix products: 48 us -> 32.1 us  [product(): return jnp.dot(left_side, right_side, preferred_element_type=jnp.float32)]
  transfers between devices with their start and end apart: 10 -> 0, of which waited for: 8 -> 0; matrix products, arithmetic and copies ran while one was open for 17% -> 0% of each run, Pallas kernels for 0% -> 0%
where the time goes in v1:
time: 539 us; the launch traced here: 530 us
  Pallas kernels  217 us (40%)
  matrix products  112 us (21%)
  local copies, waits for them, and re-layouts  92.8 us (17%)
  blocking collectives  80.3 us (15%)
  other arithmetic  26.7 us (5%)
    pallas_call x1, Pallas kernels, scatter_all(): pl.pallas_call(scatter_kernel, out_shape=(jax.ShapeDtypeStruct((12, 24, 7...  118 us
    pallas_call x1, Pallas kernels, gather_all(): pl.pallas_call(gather_kernel, out_shape=(jax.ShapeDtypeStruct((12, 4, 2,...  98.2 us
    all_gather x1, blocking collectives, shards_block(): lax.all_gather(gain_master.astype(jnp.bfloat16), axes, axis=1, tiled=True)  43.2 us
    psum x1, blocking collectives, shards_block(): lax.psum(jnp.concatenate([gg.reshape(-1), table_grad.reshape(-1)]), axes)  37 us
    dot_general x10, matrix products, product(): return jnp.dot(left_side, right_side, preferred_element_type=jnp.float32)  32.1 us
    dot_general x10, matrix products, product_over_rows(): lax.dot_general(left_side, right_side, (((0,), (0,)), ((), ())), preferre...  25.6 us
    unnamed x222, local copies, waits for them, and re-layouts  25.1 us
    reshape x8, local copies, waits for them, and re-layouts, to_heads(): return values.reshape(sequences, -1, HEADS, HEAD_DIM)  16.8 us

profile of v1, /device:TPU:0, one launch (start us, length us, event | category | flops | bytes accessed | tf_op | source)
XLA Modules:
  0.0 530.3 jit_solution(9114565937313070879)
XLA Ops:
  6.0 43.2 %all-gather = bf16[32,24,3]{1,2,0:T(4,128)(2,1)S(1)} all-gather(bf16[1,24,3]{1,2,0:T(4,128)(2,1)S(1)} %convert_bitcast_fusion), channel_id=1, replica_groups=mesh['dp'=8,'fsdp'=4] {'dp','fsdp'}, dimensions={0}, use_global_device_ids=true | all-gather | bytes 4752 | tf_op jit(solution)/shard_map/all_gather | solution.py:984
  61.6 4.1 fusion.23
  65.7 5.0 copy.220
  70.7 98.2 %shard_map.489 = (bf16[12,4,2,2,48,768]{5,4,3,2,1,0:T(8,128)(2,1)}, bf16[4,2,2,2,2,48,768]{6,5,4,3,2,1,0:T(8,128)(2,1)}) custom-call(f32[6,2,24,768]{3,2,1,0:T(8,128)} %bitcast.335, f32[96,768]{1,0:T(8,128)} %o_ref.1), custom_call_target="tpu_custom_call" | custom-call | tf_op jit(solution)/shard_map/pallas_call | solution.py:901
  168.9 9.8 %fusion.131 = (bf16[1,4,2,2,48,768]{5,4,3,2,1,0:T(8,128)(2,1)}, bf16[1,4,2,2,48,768]{5,4,3,2,1,0:T(8,128)(2,1)}, bf16[1,4,2,2,48,768]{5,4,3,2,1,0:T(8,128)(2,1)}...) fusion(bf16[12,4,2,2,48,768]{5,4,3,2,1,0:T(8,128)(2,1)} %get-tu, ...), kind=kLoop, calls=%fused_computation.230 | loop fusion | bytes 28311552 | tf_op jit(solution)/shard_map/slice | solution.py:989
  185.4 2.9 reshape.511
  188.3 2.3 convolution_convert_fusion.15
  194.0 3.2 convolution_convert_fusion.16
  201.4 2.3 copy.216
  203.7 2.4 reshape.509
  206.2 3.7 fusion.133
  218.3 2.3 copy.224
  220.6 2.9 reshape.512
  223.5 4.8 fusion.135
  237.8 10.3 %fusion.8 = (bf16[512,3072]{1,0:T(8,128)(2,1)}, f32[512,3072]{1,0:T(8,128)}) fusion(f32[512,3072]{1,0:T(8,128)S(1)} %fusion.135, bf16[768,768]{1,0:T(8,128)(2,1)S(1)} %bitcast.348, bf16[768,768]{1,0:T(8,128)(2,1)S(1)} %bitcast.350, bf16[768,768]{1,0:T(8,128)(2,1)S(1)} %bitcast.352, bf16[768,768]{1,0:T(8,128)(2,1)S(1)} %bitcast.346, ...), kind=kOutput, calls=%fused_computation.11 | convolution fusion | flops 2467430400 | bytes 22025216 | tf_op jit(solution)/shard_map/dot_general | solution.py:47
  248.2 7.6 %add_convert_fusion = bf16[512,768]{1,0:T(8,128)(2,1)} fusion(f32[512,768]{1,0:T(8,128)S(1)} %get-tuple-element.235, bf16[3072,768]{1,0:T(8,128)(2,1)S(1)} %bitcast.380, f32[512,3072]{1,0:T(8,128)} %get-tuple-element.237), kind=kOutput, calls=%fused_computation.71 | convolution fusion | flops 2430861312 | bytes 13369344 | tf_op jit(solution)/shard_map/dot_general | solution.py:47
  255.8 2.8 multiply_reduce_fusion.2
  259.3 4.6 convolution_convert_fusion.1
  265.6 4.9 convolution_convert_fusion
  270.5 2.5 copy.230
  273.0 2.9 reshape.515
  275.9 4.9 copy.353
  288.5 2.3 fusion.67
  304.2 3.8 fusion.56
  311.2 7.1 %multiply_reduce_fusion = (f32[2,12,256]{2,1,0:T(8,128)S(1)}, f32[2,12,256,256]{2,3,1,0:T(8,128)}) fusion(f32[2,12,256,256]{2,3,1,0:T(8,128)} %copy-done.1, f32[2,12,256]{2,1,0:T(8,128)S(1)} %log_add_fusion, bf16[2,256,12,64]{1,0,3,2:T(2,128)(2,1)S(1)} %copy-done.30, bf16[2,256,12,64]{1,0,3,2:T(2,128)(2,1)S(1)} %reshape.516), kind=kOutput, calls=%fused_computation.14 | convolution fusion | flops 206039040 | bytes 14204928 | tf_op jit(solution)/shard_map/sihe,sjhe->shij/dot_general | solution.py:105
  318.3 6.9 %convert_reduce_fusion = (f32[12,256,256]{1,2,0:T(8,128)}, bf16[2,12,256,256]{2,3,1,0:T(8,128)(2,1)S(1)}) fusion(f32[2,12,256,256]{2,3,1,0:T(8,128)} %get-tuple-element.242, f32[2,12,256]{2,1,0:T(8,128)S(1)} %get-tuple-element.241, f32[2,12,256,256]{2,3,1,0:T(8,128)S(1)} %bitcast.299, f32[2,12,256]{2,1,0:T(8,128)S(1)} %log_add_fusion), kind=kLoop, calls=%fused_computation.12 | loop fusion | flops 8650752 | bytes 18923520 | tf_op jit(solution)/shard_map/reduce_sum | solution.py:297
  335.2 5.2 copy.262
  340.5 6.4 %fusion.70 = f32[32,12]{1,0:T(8,128)S(1)} fusion(f32[12,256,256]{2,0,1:T(8,128)} %copy.262, s32[256,256]{1,0:T(8,128)S(1)} %copy-done.41), kind=kOutput, calls=%fused_computation.121 | convolution fusion | flops 304087040 | bytes 3409408 | tf_op jit(solution)/shard_map/bij,hij->bh/dot_general | solution.py:1007
  347.0 37.0 %psum.7 = f32[2688]{0:T(1024)S(1)} all-reduce(f32[2688]{0:T(1024)S(1)} %pad_maximum_fusion.7), channel_id=1, replica_groups=mesh['dp'=8,'fsdp'=4] {'dp','fsdp'}, use_global_device_ids=true, to_apply=%region_16.17 | all-reduce | flops 2688 | bytes 21504 | tf_op jit(solution)/shard_map/psum | solution.py:1008
  385.6 3.2 fusion.37
  400.3 2.5 constant_dynamic-update-slice_fusion.ga_in
  402.8 118.5 %shard_map.490 = (f32[12,24,768]{2,1,0:T(8,128)}, f32[8,48,768]{2,1,0:T(8,128)}) custom-call(bf16[12,4,2,2,48,768]{5,4,3,2,1,0:T(8,128)(2,1)} %constant_dynamic-update-slice_fusion.ga_in, bf16[4,2,2,2,2,48,768]{6,5,4,3,2,1,0:T(8,128)(2,1)} %bitcast.314), custom_call_target="tpu_custom_call" | custom-call | tf_op jit(solution)/shard_map/pallas_call | solution.py:945
  (323 shorter events, 107.4 us)
Async XLA Ops:
  3.2 50.0 %copy-start.37 = (bf16[2,1,256,768]{3,2,1,0:T(8,128)(2,1)S(1)}, bf16[2,1,256,768]{3,2,1,0:T(8,128)(2,1)}, u32[]{:S(2)}) copy-start(bf16[2,1,256,768]{3,2,1,0:T(8,128)(2,1)} %param.28) | copy-start | bytes 2359300
  50.5 11.0 %copy-start.40 = (s32[256,256]{1,0:T(8,128)}, s32[256,256]{1,0:T(8,128)S(1)}, u32[]{:S(2)}) copy-start(s32[256,256]{1,0:T(8,128)S(1)} %compare_select_fusion) | copy-start | bytes 786436
  52.0 9.5 %copy-start.35 = (bf16[2,1,256,768]{3,2,1,0:T(8,128)(2,1)}, bf16[2,1,256,768]{3,2,1,0:T(8,128)(2,1)S(1)}, u32[]{:S(2)}) copy-start(bf16[2,1,256,768]{3,2,1,0:T(8,128)(2,1)S(1)} %fusion.34) | copy-start | bytes 2359300
  52.0 9.6 %copy-start.82 = (f32[32,12]{0,1:T(8,128)S(1)}, f32[32,12]{0,1:T(8,128)}, u32[]{:S(2)}) copy-start(f32[32,12]{0,1:T(8,128)} %param.37) | copy-start | bytes 4612
  61.5 9.1 %copy-start.42 = (f32[12,24,768]{2,1,0:T(8,128)}, f32[12,24,768]{2,1,0:T(8,128)S(1)}, u32[]{:S(2)}) copy-start(f32[12,24,768]{2,1,0:T(8,128)S(1)} %fusion.104) | copy-start | bytes 2654212
  178.7 5.0 copy-start.22
  183.7 44.6 %copy-start.18 = (bf16[2,256,12,64]{1,0,3,2:T(2,128)(2,1)}, bf16[2,256,12,64]{1,0,3,2:T(2,128)(2,1)S(1)}, u32[]{:S(2)}) copy-start(bf16[2,256,12,64]{1,0,3,2:T(2,128)(2,1)S(1)} %reshape.513) | copy-start | bytes 2359300
  194.0 12.1 %copy-start.14 = (bf16[2,256,12,64]{1,0,3,2:T(2,128)(2,1)}, bf16[2,256,12,64]{1,0,3,2:T(2,128)(2,1)S(1)}, u32[]{:S(2)}) copy-start(bf16[2,256,12,64]{1,0,3,2:T(2,128)(2,1)S(1)} %reshape.510) | copy-start | bytes 2359300
  200.3 5.8 %copy-start.69 = (pred[2,256,256]{1,2,0:T(8,128)(4,1)S(1)}, pred[2,256,256]{1,2,0:T(8,128)(4,1)}, u32[]{:S(2)}) copy-start(pred[2,256,256]{1,2,0:T(8,128)(4,1)} %broadcast_and_fusion) | copy-start | bytes 393220
  216.2 19.0 %copy-start.8 = (f32[512,768]{1,0:T(8,128)}, f32[512,768]{1,0:T(8,128)S(1)}, u32[]{:S(2)}) copy-start(f32[512,768]{1,0:T(8,128)S(1)} %get-tuple-element.231) | copy-start | bytes 4718596
  223.5 4.8 copy-start.20
  235.5 12.7 %slice-start.6 = ((s8[4718592]{0:T(1024)(128)(4,1)}), s8[4194304]{0:T(1024)(128)(4,1)S(1)}, s32[]{:S(2)}) async-start(s8[4718592]{0:T(1024)(128)(4,1)} %bitcast.378), calls=%async_computation.6 | async-start | bytes 8388608
  237.8 10.3 %slice-start.7 = ((s8[4718592]{0:T(1024)(128)(4,1)}), s8[524288]{0:T(1024)(128)(4,1)S(1)}, s32[]{:S(2)}) async-start(s8[4718592]{0:T(1024)(128)(4,1)} %bitcast.378), calls=%async_computation.7 | async-start | bytes 1048576
  248.1 7.6 %copy-start.90 = (bf16[512,3072]{1,0:T(8,128)(2,1)S(1)}, bf16[512,3072]{1,0:T(8,128)(2,1)}, u32[]{:S(2)}) copy-start(bf16[512,3072]{1,0:T(8,128)(2,1)} %get-tuple-element.236) | copy-start | bytes 9437188
  258.6 6.9 %slice-start.8 = ((s8[6291456]{0:T(1024)(128)(4,1)}), s8[4194304]{0:T(1024)(128)(4,1)S(1)}, s32[]{:S(2)}) async-start(s8[6291456]{0:T(1024)(128)(4,1)} %bitcast.383), calls=%async_computation.8 | async-start | bytes 8388608
  259.2 4.6 copy-start.3
  259.2 6.3 %slice-start.9 = ((s8[6291456]{0:T(1024)(128)(4,1)}), s8[2097152]{0:T(1024)(128)(4,1)S(1)}, s32[]{:S(2)}) async-start(s8[6291456]{0:T(1024)(128)(4,1)} %bitcast.383), calls=%async_computation.9 | async-start | bytes 4194304
  270.5 10.3 %slice-start.2 = ((s8[6291456]{0:T(1024)(128)(4,1)}), s8[2097152]{0:T(1024)(128)(4,1)S(1)}, s32[]{:S(2)}) async-start(s8[6291456]{0:T(1024)(128)(4,1)} %bitcast.300), calls=%async_computation.2 | async-start | bytes 4194304
  275.9 4.9 slice-start.3
  275.9 4.9 copy-start.21
  311.2 7.1 %slice-start = ((s8[6291456]{0:T(1024)(128)(4,1)}), s8[4194304]{0:T(1024)(128)(4,1)S(1)}, s32[]{:S(2)}) async-start(s8[6291456]{0:T(1024)(128)(4,1)} %bitcast.298), calls=%async_computation | async-start | bytes 8388608
  311.2 7.1 %slice-start.1 = ((s8[6291456]{0:T(1024)(128)(4,1)}), s8[2097152]{0:T(1024)(128)(4,1)S(1)}, s32[]{:S(2)}) async-start(s8[6291456]{0:T(1024)(128)(4,1)} %bitcast.298), calls=%async_computation.1 | async-start | bytes 4194304
  318.3 6.9 %copy-start.17 = (bf16[2,256,12,64]{1,0,3,2:T(2,128)(2,1)S(1)}, bf16[2,256,12,64]{1,0,3,2:T(2,128)(2,1)}, u32[]{:S(2)}) copy-start(bf16[2,256,12,64]{1,0,3,2:T(2,128)(2,1)} %copy-done.16) | copy-start | bytes 2359300
  335.2 5.2 copy-start.41
  340.4 43.6 %copy-start.87 = (f32[3,24]{1,0:T(4,128)S(1)}, f32[3,24]{1,0:T(4,128)}, u32[]{:S(2)}) copy-start(f32[3,24]{1,0:T(4,128)} %param.36) | copy-start | bytes 868
  340.4 43.6 %copy-start.88 = (f32[3,24]{1,0:T(4,128)S(1)}, f32[3,24]{1,0:T(4,128)}, u32[]{:S(2)}) copy-start(f32[3,24]{1,0:T(4,128)} %param.43) | copy-start | bytes 868
  340.4 43.6 %copy-start.89 = (f32[3,24]{1,0:T(4,128)S(1)}, f32[3,24]{1,0:T(4,128)}, u32[]{:S(2)}) copy-start(f32[3,24]{1,0:T(4,128)} %param.50) | copy-start | bytes 868
  340.5 44.5 %copy-start.83 = (f32[32,12]{0,1:T(8,128)S(1)}, f32[32,12]{0,1:T(8,128)}, u32[]{:S(2)}) copy-start(f32[32,12]{0,1:T(8,128)} %param.37) | copy-start | bytes 4612
  340.5 44.5 %copy-start.85 = (f32[32,12]{0,1:T(8,128)S(1)}, f32[32,12]{0,1:T(8,128)}, u32[]{:S(2)}) copy-start(f32[32,12]{0,1:T(8,128)} %param.44) | copy-start | bytes 4612
  340.5 44.5 %copy-start.86 = (f32[32,12]{0,1:T(8,128)S(1)}, f32[32,12]{0,1:T(8,128)}, u32[]{:S(2)}) copy-start(f32[32,12]{0,1:T(8,128)} %param.51) | copy-start | bytes 4612
  392.5 7.8 %slice-start.4 = ((s8[4718592]{0:T(1024)(128)(4,1)}), s8[4194304]{0:T(1024)(128)(4,1)S(1)}, s32[]{:S(2)}) async-start(s8[4718592]{0:T(1024)(128)(4,1)} %bitcast.302), calls=%async_computation.4 | async-start | bytes 8388608
  395.4 4.8 slice-start.5
  (69 other events, 163.9 us)

commit v2 on v1

--- a/solution.py
+++ b/solution.py
@@ -600,11 +600,12 @@
         self.k, self.f = place, f
         self.send, self.recv = send, recv
         self.first_cross = ORDERS[f][0] == "a"
-        self.stages = [self.start, self.cross if self.first_cross else (lambda: self.step(1)),
-                       (lambda: self.step(1 if self.first_cross else 2)),
-                       (lambda: self.step(2 if self.first_cross else 3)),
-                       (lambda: self.step(3)) if self.first_cross else self.cross,
-                       self.second, self.finish]
+
+    def do(self, name):
+        if name[0] in "LR":
+            self.step(int(name[1]), name[0])
+        else:
+            getattr(self, name)()
 
     def blk(self, zi):
         p, q = self.k.own(self.f)
@@ -654,30 +655,31 @@
 
         self.sideways(zi)
 
-    def step(self, t):
+    def step(self, t, side):
         z = self.k.z
 
-        @pl.when(z >= t)
-        def _():
-            got(self.k, self.blk(z - t), self.recv.at[self.f, t], "l")
-
-            if t < 3:
-                @pl.when(z < 3)
-                def _():
-                    self.move(self.blk(z - t), 1, t + 1, "r")
-
-            self.sideways(z - t)
-
-        @pl.when(z <= 3 - t)
-        def _():
-            got(self.k, self.blk(z + t), self.recv.at[self.f, 3 + t], "r")
-
-            if t < 3:
-                @pl.when(z > 0)
-                def _():
-                    self.move(self.blk(z + t), 2, 3 + t + 1, "l")
-
-            self.sideways(z + t)
+        if side == "L":
+            @pl.when(z >= t)
+            def _():
+                got(self.k, self.blk(z - t), self.recv.at[self.f, t], "l")
+
+                if t < 3:
+                    @pl.when(z < 3)
+                    def _():
+                        self.move(self.blk(z - t), 1, t + 1, "r")
+
+                self.sideways(z - t)
+        else:
+            @pl.when(z <= 3 - t)
+            def _():
+                got(self.k, self.blk(z + t), self.recv.at[self.f, 3 + t], "r")
+
+                if t < 3:
+                    @pl.when(z > 0)
+                    def _():
+                        self.move(self.blk(z + t), 2, 3 + t + 1, "l")
+
+                self.sideways(z + t)
 
     def second(self):
         p, q = self.k.own(self.f)
@@ -731,16 +733,19 @@
 
 
 class Scatter:
-    def __init__(self, place, f, send, recv, slots, final, result):
+    def __init__(self, place, f, send, recv, slots, final, result, credit):
         self.k, self.f = place, f
+        self.wait_credit, self.give_credit, self.credit = credit
         self.send, self.recv = send, recv
         self.rd, self.rq, self.rp, self.rl, self.rr = slots
         self.final, self.result = final, result
         self.wide = ORDERS[f][0] == "a"
-        self.stages = [self.start, self.core, self.half,
-                       *([] if self.wide else [self.cross_in]),
-                       (lambda: self.step_in(1)), (lambda: self.step_in(2)), (lambda: self.step_in(3)),
-                       *([self.last] if self.wide else []), self.finish]
+
+    def do(self, name):
+        if name[0] == "z":
+            self.step_in(int(name[1]))
+        else:
+            getattr(self, name)()
 
     def move(self, src, dst, s, way):
         push(self.k, src, dst, self.send.at[self.f, s], self.recv.at[self.f, s], way)
@@ -750,6 +755,8 @@
         return self.k.pick(self.f, zi, ALL if self.wide else p, q)
 
     def start(self):
+        if self.wait_credit:
+            pl.semaphore_wait(self.credit, 1)
         self.move(self.k.pick(self.f, ALL, ALL, ALL, 1 - self.k.c), self.rd, 0, "c")
 
     def rpick(self, ps, qs):
@@ -769,6 +776,8 @@
         pw, qw = self.k.ways(self.f)
         got(self.k, self.rq, self.recv.at[self.f, 1], qw)
         add_into(self.k.pick(self.f, ALL, ALL, q), [self.rpick(ALL, q), self.rq], (4, 2))
+        if self.give_credit:
+            pl.semaphore_signal(self.credit, inc=1, device_id=self.k.to["c"], device_id_type=MESH)
         if self.wide:
             self.step_out(1)
         else:
@@ -859,111 +868,580 @@
             left_out(k, self.final.at[pl.ds(0, 24)], self.send.at[f, 9], "c")
 
 
-def weave(flows, gap=0):
-    out = []
-    rounds = max(i * gap + len(flow.stages) for i, flow in enumerate(flows))
-    for r in range(rounds):
-        for i, flow in enumerate(flows):
-            s = r - i * gap
-            if 0 <= s < len(flow.stages):
-                out.append(flow.stages[s])
-    return out
-
-
-def gather_kernel(m_ref, o_ref, wa, wf, xch, send, recv, xs, xr):
+class Line:
+    def __init__(self, place, buf, send, recv):
+        self.k, self.buf, self.send, self.recv = place, buf, send, recv
+
+    def move(self, zi, s, r, way):
+        push(self.k, self.buf.at[zi], self.buf.at[zi], self.send.at[s], self.recv.at[r], way)
+
+    def start(self):
+        z = self.k.z
+
+        @pl.when(z < 3)
+        def _():
+            self.move(z, 3, 3, "r")
+
+        @pl.when(z > 0)
+        def _():
+            self.move(z, 6, 6, "l")
+
+    def step(self, t):
+        z = self.k.z
+
+        @pl.when(z >= t)
+        def _():
+            got(self.k, self.buf.at[z - t], self.recv.at[2 + t], "l")
+
+            if t < 3:
+                @pl.when(z < 3)
+                def _():
+                    self.move(z - t, 3 + t, 3 + t, "r")
+
+        @pl.when(z <= 3 - t)
+        def _():
+            got(self.k, self.buf.at[z + t], self.recv.at[5 + t], "r")
+
+            if t < 3:
+                @pl.when(z > 0)
+                def _():
+                    self.move(z + t, 6 + t, 6 + t, "l")
+
+    def drain(self):
+        z = self.k.z
+        for t in range(3):
+            @pl.when((z < 3) & (z >= t))
+            def _():
+                left_out(self.k, self.buf.at[0], self.send.at[3 + t], "r")
+
+            @pl.when((z > 0) & (z <= 3 - t))
+            def _():
+                left_out(self.k, self.buf.at[0], self.send.at[6 + t], "l")
+
+
+class Gains:
+    def __init__(self, place, buf, send, recv):
+        self.k, self.buf, self.send, self.recv = place, buf, send, recv
+        self.line = Line(place, buf, send, recv)
+        z, y, x, c = place.z, place.y, place.x, place.c
+        self.mine = [buf.at[z, y, x, c], buf.at[z, y, x], buf.at[z, y]]
+        self.other = [buf.at[z, y, x, 1 - c], buf.at[z, y, 1 - x], buf.at[z, 1 - y]]
+
+    def go(self, i):
+        if 1 <= i <= 3:
+            got(self.k, self.other[i - 1], self.recv.at[i - 1], "cxy"[i - 1])
+        if i < 3:
+            push(self.k, self.mine[i], self.mine[i], self.send.at[i], self.recv.at[i], "cxy"[i])
+        elif i == 3:
+            self.line.start()
+        else:
+            self.line.step(i - 3)
+
+    def drain(self):
+        for i in range(3):
+            left_out(self.k, self.mine[i], self.send.at[i], "cxy"[i])
+        self.line.drain()
+
+
+class Small:
+    def __init__(self, place, bufs, got_bufs, along, send, recv):
+        self.k, self.bufs, self.got_bufs, self.along = place, bufs, got_bufs, along
+        self.send, self.recv = send, recv
+        self.line = Line(place, along, send, recv)
+
+    def go(self, i):
+        if 1 <= i <= 3:
+            got(self.k, self.got_bufs.at[i - 1], self.recv.at[i - 1], "cxy"[i - 1])
+            total = self.bufs[i - 1] + self.got_bufs[i - 1]
+            if i < 3:
+                self.bufs[i] = total
+            else:
+                self.along[self.k.z] = total
+        if i < 3:
+            push(self.k, self.bufs.at[i], self.got_bufs.at[i], self.send.at[i], self.recv.at[i], "cxy"[i])
+        elif i == 3:
+            self.line.start()
+        else:
+            self.line.step(i - 3)
+
+    def drain(self):
+        for i in range(3):
+            left_out(self.k, self.bufs.at[i], self.send.at[i], "cxy"[i])
+        self.line.drain()
+BF, F32 = jnp.bfloat16, jnp.float32
+ROOT = math.sqrt(2.0 / math.pi)
+CUBE = 0.044715
+
+
+def dot_nn(a, b):
+    return lax.dot_general(a, b, (((1,), (0,)), ((), ())), preferred_element_type=F32)
+
+
+def dot_nt(a, b):
+    return lax.dot_general(a, b, (((1,), (1,)), ((), ())), preferred_element_type=F32)
+
+
+def dot_tn(a, b):
+    return lax.dot_general(a, b, (((0,), (0,)), ((), ())), preferred_element_type=F32)
+
+
+def unit_of(values):
+    scale = lax.rsqrt(jnp.mean(values * values, axis=-1, keepdims=True) + epsilon_norm)
+    return values * scale, scale
+
+
+class Layer:
+    def __init__(self, wa, wf, b):
+        self.wa, self.wf, self.b = wa, wf, b
+
+    def cols(self, u, t):
+        return self.wa[u, :, :, :, :, pl.ds(pl.multiple_of(256 * t, 256), 256)].reshape(768, 256)
+
+    def half_rows(self, u, t):
+        return self.wa[u, pl.ds(2 * t, 2)].reshape(384, 768)
+
+    def times(self, a, u, put):
+        def body(t, _):
+            put(pl.ds(pl.multiple_of(256 * t, 256), 256), dot_nn(a[...], self.cols(u, t)))
+            return 0
+
+        lax.fori_loop(0, 3, body, 0)
+
+    def times_back(self, pairs, put):
+        def body(t, _):
+            total = None
+            for a, u in pairs:
+                term = dot_nt(a[...], self.half_rows(u, t))
+                total = term if total is None else total + term
+            put(pl.ds(pl.multiple_of(384 * t, 384), 384), total)
+            return 0
+
+        lax.fori_loop(0, 2, body, 0)
+
+    def weight_grad(self, a, d, u):
+        def body(t, _):
+            tile = a[:, pl.ds(pl.multiple_of(384 * t, 384), 384)]
+            self.wa[u, pl.ds(2 * t, 2)] = dot_tn(tile, d[...]).astype(BF).reshape(2, 2, 2, 48, 768)
+            return 0
+
+        lax.fori_loop(0, 2, body, 0)
+
+    def project(self, a, u, dst):
+        def put(tile, value):
+            dst[:, tile] = value.astype(BF)
+
+        self.times(a, u, put)
+
+    def add_project(self, base, a, u, dst):
+        def put(tile, value):
+            dst[:, tile] = base[:, tile].astype(F32) + value
+
+        self.times(a, u, put)
+
+    def norm(self, src, g, dst):
+        gain = self.b["gain"][pl.ds(g, 1), :]
+
+        def body(i, _):
+            rows = pl.ds(pl.multiple_of(64 * i, 64), 64)
+            unit, _unused = unit_of(src[rows].astype(F32))
+            dst[rows] = (unit * gain).astype(BF)
+            return 0
+
+        lax.fori_loop(0, 8, body, 0)
+
+    def norm_back(self, dn, src, g, base, dst, low):
+        gain = self.b["gain"][pl.ds(g, 1), :]
+
+        def body(i, acc):
+            rows = pl.ds(pl.multiple_of(64 * i, 64), 64)
+            unit, scale = unit_of(src[rows].astype(F32))
+            grad = dn[rows]
+            acc = acc + jnp.sum(grad * unit, axis=0, keepdims=True)
+            pulled = grad * gain
+            value = base(rows, i) + scale * (pulled - unit * jnp.mean(pulled * unit, axis=-1, keepdims=True))
+            dst[rows] = value
+            if low is not None:
+                low[rows] = value.astype(BF)
+            return acc
+
+        total = lax.fori_loop(0, 8, body, jnp.zeros((1, 768), F32))
+        for i in range(3):
+            self.b["small"][3 * g + i:3 * g + i + 1, :] = total[:, 256 * i:256 * i + 256]
+
+    def head_masks(self):
+        lane = lax.broadcasted_iota(jnp.int32, (1, 128), 1)
+        low = (lane < 64).astype(F32)
+        return low.astype(BF), (1.0 - low).astype(BF)
+
+    def allowed(self, s, kind):
+        row = lax.broadcasted_iota(jnp.int32, (256, 256), 0)
+        col = lax.broadcasted_iota(jnp.int32, (256, 256), 1)
+        if kind == 1:
+            return (col <= row) & (col < self.b["lens"][s])
+        return col < self.b["lens"][2 + s]
+
+    def bias(self, head):
+        row = self.b["bias_row"][pl.ds(head, 1), :]
+        return pltpu.roll(jnp.broadcast_to(row, (256, 256)), 0, axis=1, stride=1, stride_axis=0)
+
+    def weights(self, queries, keys, bias, allowed):
+        scores = dot_nt(queries, keys) * score_scale
+        if bias is not None:
+            scores = scores + bias
+        scores = jnp.where(allowed, scores, masked_score)
+        expanded = jnp.exp(scores - jnp.max(scores, axis=-1, keepdims=True))
+        return expanded / jnp.sum(expanded, axis=-1, keepdims=True)
+
+    def attend(self, kind, first, last):
+        b = self.b
+        q, k, v, o = (b[n + str(kind)] for n in "qkvo")
+        masks = self.head_masks()
+        keep = masks[0].astype(F32)
+
+        def body(i, _):
+            hp, s = i // 2, i % 2
+            lanes = pl.ds(pl.multiple_of(128 * hp, 128), 128)
+            rows = pl.ds(pl.multiple_of(256 * s, 256), 256)
+            queries, keys, values = q[rows, lanes], k[rows, lanes], v[rows, lanes]
+            allowed = self.allowed(s, kind)
+            mixed = []
+            for e in range(2):
+                bias = self.bias(2 * hp + e) if kind == 1 else None
+                p = self.weights(queries * masks[e], keys, bias, allowed)
+                mixed.append(dot_nn(p.astype(BF), values))
+            o[rows, lanes] = (mixed[0] * keep + mixed[1] * (1.0 - keep)).astype(BF)
+            return 0
+
+        lax.fori_loop(2 * first, 2 * last, body, 0)
+
+    def attend_back(self, kind, first, last):
+        b = self.b
+        q, k, v = (b[n + str(kind)] for n in "qkv")
+        masks = self.head_masks()
+        row = lax.broadcasted_iota(jnp.int32, (256, 256), 0)
+        col = lax.broadcasted_iota(jnp.int32, (256, 256), 1)
+        flip = (row + col == 255).astype(F32).astype(BF)
+
+        def body(i, _):
+            hp, s = i // 2, i % 2
+            lanes = pl.ds(pl.multiple_of(128 * hp, 128), 128)
+            rows = pl.ds(pl.multiple_of(256 * s, 256), 256)
+            queries, keys, values = q[rows, lanes], k[rows, lanes], v[rows, lanes]
+            given = b["do"][rows, lanes]
+            allowed = self.allowed(s, kind)
+            dq = dk = dv = None
+            for e in range(2):
+                bias = self.bias(2 * hp + e) if kind == 1 else None
+                qe = queries * masks[e]
+                ge = given * masks[e]
+                p = self.weights(qe, keys, bias, allowed)
+                dp = dot_nt(ge, values)
+                ds = (p * (dp - jnp.sum(p * dp, axis=-1, keepdims=True))).astype(BF)
+                if kind == 1:
+                    turned = pltpu.roll(dot_nn(flip, ds), 0, axis=1, stride=1, stride_axis=0)
+                    b["small"][pl.ds(9 + 2 * hp + e, 1), :] += jnp.sum(turned, axis=0, keepdims=True)
+                terms = (dot_nn(ds, keys * masks[e]), dot_tn(ds, qe), dot_tn(p.astype(BF), ge))
+                if dq is None:
+                    dq, dk, dv = terms
+                else:
+                    dq, dk, dv = dq + terms[0], dk + terms[1], dv + terms[2]
+            q[rows, lanes] = (dq * score_scale).astype(BF)
+            k[rows, lanes] = (dk * score_scale).astype(BF)
+            v[rows, lanes] = dv.astype(BF)
+            return 0
+
+        lax.fori_loop(2 * first, 2 * last, body, 0)
+
+    def live(self, i):
+        row = lax.broadcasted_iota(jnp.int32, (64, 1), 0) + 64 * lax.rem(i, 4)
+        bound = jnp.where(i < 4, self.b["lens"][0], self.b["lens"][1])
+        return (row < bound).astype(F32)
+
+    def cotangent(self):
+        b = self.b
+
+        def body(i, _):
+            rows = pl.ds(pl.multiple_of(64 * i, 64), 64)
+            b["df"][rows] = (b["cot"][rows].astype(F32) * self.live(i)).astype(BF)
+            return 0
+
+        lax.fori_loop(0, 8, body, 0)
+
+    def ffn_act(self, j):
+        b = self.b
+
+        def body(t, _):
+            cols = pl.ds(pl.multiple_of(384 * t, 384), 384)
+            wi = self.wa[8 + j, :, :, :, :, cols].reshape(768, 384)
+            wf = self.wf[j, t].reshape(384, 768)
+            u = dot_nn(b["n3"][...], wi)
+            square = u * u
+            th = jnp.tanh(ROOT * (u + CUBE * (u * square)))
+            half = 0.5 * (1.0 + th)
+            b["act"][:, cols] = (u * half).astype(BF)
+            slope = half + (0.5 * ROOT) * u * (1.0 - th * th) * (1.0 + (3.0 * CUBE) * square)
+            da = dot_nt(b["df"][...], wf)
+            b["du"][:, cols] = (da * slope).astype(BF)
+            return 0
+
+        lax.fori_loop(0, 2, body, 0)
+
+    def ffn_out(self, j):
+        b = self.b
+
+        def body(t, _):
+            cols = pl.ds(pl.multiple_of(256 * t, 256), 256)
+            wf = self.wf[j, :, :, :, :, :, cols].reshape(768, 256)
+            b["y"][:, cols] += dot_nn(b["act"][...], wf)
+            return 0
+
+        lax.fori_loop(0, 3, body, 0)
+
+    def ffn_back(self, j):
+        b = self.b
+
+        def put(tile, value):
+            if j == 0:
+                b["dn"][:, tile] = value
+            else:
+                b["dn"][:, tile] += value
+
+        self.times_back([(b["du"], 8 + j)], put)
+
+    def ffn_grads(self, j):
+        b = self.b
+
+        def body(t, _):
+            tile = b["act"][:, pl.ds(pl.multiple_of(384 * t, 384), 384)]
+            self.wf[j, t] = dot_tn(tile, b["df"][...]).astype(BF).reshape(2, 2, 2, 48, 768)
+            return 0
+
+        lax.fori_loop(0, 2, body, 0)
+        self.weight_grad(b["n3"], b["du"], 8 + j)
+
+
+SCATTER_ORDER = (4, 5, 6, 7, 3, 2, 1, 0)
+
+
+def layer_kernel(
+    program, lens, hid, mem, cot, masters, outer, gain_tile, spread, owner, bias_row,
+    low_out, hidden_grad, memory_grad, res, last, small_out,
+    wa, wf, n1, q1, k1, v1, o1, n2, q2, k2, v2, o2, n3, act, du, df, x1, x2, dn,
+    rd, rq, rlw, rrw, rpw, rln, rrn, rpn, fin, tiles, gain, small, small_got, along,
+    gs, gr, ss, sr, xs, xr, ks, kr, ms, mr, credit,
+):
     k = Place(wa, wf)
-    k.enter()
     z, y, x, c = k.z, k.y, k.x, k.c
-    row = pl.ds(pl.multiple_of(24 * c, 8), 24)
-    push(k, m_ref.at[:, 1 - c], xch.at[:, row], xs, xr, "c")
-    for h in range(2):
-        wf[z, y, x, c, h] = o_ref[48 * h:48 * h + 48].astype(jnp.bfloat16)
-    flows = [Gather(k, f, send, recv) for f in range(8)]
-    for f in (6, 7):
-        flows[f].start()
-    for p in range(PAIRS):
-        xch[p, row] = m_ref[p, c]
+    b = dict(
+        lens=lens, hid=hid, mem=mem, cot=cot, bias_row=bias_row, gain=gain, small=small.at[0],
+        n1=n1, q1=q1, k1=k1, v1=v1, o1=o1, n2=n2, q2=q2, k2=k2, v2=v2, o2=o2, n3=n3,
+        act=act, du=du, df=df, do=act, y=memory_grad, dn=dn,
+    )
+    net = Layer(wa, wf, b)
+    gathers = [Gather(k, f, gs, gr) for f in range(8)]
+    scatters = {}
+    for i, f in enumerate(SCATTER_ORDER):
+        if f < PAIRS:
+            slots = (rd.at[i % 4], rq.at[f], rpw.at[f], rlw.at[f], rrw.at[f])
+        else:
+            slots = (rd.at[i % 4], rq.at[f], rpn.at[f - PAIRS], rln.at[f - PAIRS], rrn.at[f - PAIRS])
+        final = fin.at[f] if f < PAIRS else last.at[f - PAIRS]
+        scatters[f] = Scatter(k, f, ss, sr, slots, final, res, (i >= 4, i < 4, credit))
+    gains = Gains(k, tiles, ks, kr)
+    sums = Small(k, small, small_got, along, ms, mr)
+    mine = pl.ds(pl.multiple_of(24 * c, 8), 24)
     other = pl.ds(pl.multiple_of(24 - 24 * c, 8), 24)
-    got(k, xch.at[:, other], xr, "c")
-    for p in range(PAIRS):
-        wa[2 * p + c, z, y, x] = xch[p].astype(jnp.bfloat16)
-        flows[p].start()
-    left_out(k, m_ref.at[:, 1 - c], xs, "c")
-    for flow in flows:
-        flow.stages = flow.stages[1:]
-    for stage in weave(flows):
-        stage()
-    for flow in flows:
-        flow.drain()
-
-
-def gather_all(m, o):
+
+    def enter():
+        k.enter()
+        push(k, masters.at[:, 1 - c], fin.at[:, mine], xs, xr, "c")
+        tiles[z, y, x, c] = gain_tile[...].astype(BF).astype(F32)
+        gains.go(0)
+        for h in range(2):
+            wf[z, y, x, c, h] = outer[48 * h:48 * h + 48].astype(BF)
+        for p in range(PAIRS):
+            fin[p, mine] = masters[p, c]
+
+    def swap():
+        got(k, fin.at[:, other], xr, "c")
+
+    def own(f):
+        if f < PAIRS:
+            wa[2 * f + c, z, y, x] = fin[f].astype(BF)
+        gathers[f].start()
+
+    def spread_gains():
+        flat = tiles[...].reshape(32, 8, 128)
+        for g in range(3):
+            lanes = dot_nn(flat[:, g].astype(BF), spread[...])
+            gain[g:g + 1, :] = jnp.sum(lanes * owner[...], axis=0, keepdims=True)
+
+    def put_do(tile, value):
+        act[:, tile] = value.astype(BF)
+
+    def put_dn(tile, value):
+        dn[:, tile] = value
+
+    def put_memory(tile, value):
+        memory_grad[:, tile] = value
+
+    def begin():
+        memory_grad[...] = x2[...]
+        small[0] = jnp.zeros_like(small[0])
+        net.cotangent()
+
+    def finish_low():
+        low_out[...] = memory_grad[...].astype(BF)
+
+    def total_small():
+        small_out[...] = along[0] + along[1] + along[2] + along[3]
+
+    grad = hidden_grad
+    tasks = {
+        "gain": spread_gains,
+        "n1": lambda: net.norm(hid, 0, n1),
+        "q1": lambda: net.project(n1, 0, q1),
+        "k1": lambda: net.project(n1, 1, k1),
+        "v1": lambda: net.project(n1, 2, v1),
+        "o1": lambda: net.add_project(hid, o1, 3, x1),
+        "n2": lambda: net.norm(x1, 1, n2),
+        "k2": lambda: net.project(mem, 4, k2),
+        "v2": lambda: net.project(mem, 5, v2),
+        "q2": lambda: net.project(n2, 6, q2),
+        "o2": lambda: net.add_project(x1, o2, 7, x2),
+        "n3": lambda: net.norm(x2, 2, n3),
+        "begin": begin,
+        "low": finish_low,
+        "nb3": lambda: net.norm_back(dn, x2, 2, lambda rows, i: cot[rows].astype(F32) * net.live(i), grad, df),
+        "do2": lambda: net.times_back([(df, 7)], put_do),
+        "w7": lambda: net.weight_grad(o2, df, 7),
+        "dn2": lambda: net.times_back([(q2, 6)], put_dn),
+        "w6": lambda: net.weight_grad(n2, q2, 6),
+        "mg": lambda: net.times_back([(k2, 4), (v2, 5)], put_memory),
+        "w4": lambda: net.weight_grad(mem, k2, 4),
+        "w5": lambda: net.weight_grad(mem, v2, 5),
+        "nb2": lambda: net.norm_back(dn, x1, 1, lambda rows, i: grad[rows], grad, df),
+        "do1": lambda: net.times_back([(df, 3)], put_do),
+        "w3": lambda: net.weight_grad(o1, df, 3),
+        "dn1": lambda: net.times_back([(q1, 0), (k1, 1), (v1, 2)], put_dn),
+        "w0": lambda: net.weight_grad(n1, q1, 0),
+        "w1": lambda: net.weight_grad(n1, k1, 1),
+        "w2": lambda: net.weight_grad(n1, v1, 2),
+        "nb1": lambda: net.norm_back(dn, hid, 0, lambda rows, i: grad[rows], grad, None),
+    }
+    families = {
+        "act": net.ffn_act, "out": net.ffn_out, "back": net.ffn_back, "grads": net.ffn_grads,
+        "A1": lambda i: net.attend(1, 2 * i, 2 * i + 2),
+        "A2": lambda i: net.attend(2, 2 * i, 2 * i + 2),
+        "B1": lambda i: net.attend_back(1, 2 * i, 2 * i + 2),
+        "B2": lambda i: net.attend_back(2, 2 * i, 2 * i + 2),
+    }
+    enter()
+    for kind, index, name in program:
+        if kind == "G":
+            if name == "own":
+                own(index)
+            else:
+                gathers[index].do(name)
+        elif kind == "S":
+            scatters[index].do(name)
+        elif kind == "K":
+            gains.go(index)
+        elif kind == "R":
+            if index < 7:
+                sums.go(index)
+            else:
+                total_small()
+        elif kind == "X":
+            swap()
+        elif name in tasks:
+            tasks[name]()
+        else:
+            families[name](index)
+    left_out(k, masters.at[:, 1 - c], xs, "c")
+    gains.drain()
+    sums.drain()
+    for f in SCATTER_ORDER:
+        scatters[f].drain()
+
+
+def run_layer(program, lens, hid, mem, cot, masters, outer, gain_tile, spread, owner, bias_row):
+    vm, sm = pl.BlockSpec(memory_space=pltpu.VMEM), pl.BlockSpec(memory_space=pltpu.SMEM)
+    low, wide = pltpu.VMEM((512, 768), BF), pltpu.VMEM((512, 768), F32)
+    dma = pltpu.SemaphoreType.DMA
+    shape = jax.ShapeDtypeStruct
     return pl.pallas_call(
-        gather_kernel,
-        out_shape=(jax.ShapeDtypeStruct((12, 4, 2, 2, 48, 768), jnp.bfloat16),
-                   jax.ShapeDtypeStruct((4, 2, 2, 2, 2, 48, 768), jnp.bfloat16)),
-        in_specs=[pl.BlockSpec(memory_space=pltpu.VMEM)] * 2,
-        out_specs=[pl.BlockSpec(memory_space=pltpu.VMEM)] * 2,
+        functools.partial(layer_kernel, program),
+        out_shape=(
+            shape((512, 768), BF), shape((512, 768), F32), shape((512, 768), F32),
+            shape((12, 24, 768), F32), shape((2, 48, 768), F32), shape((24, 256), F32),
+        ),
+        in_specs=[sm] + [vm] * 9,
+        out_specs=[vm] * 6,
         scratch_shapes=[
-            pltpu.VMEM((6, 48, 768), jnp.float32),
-            pltpu.SemaphoreType.DMA((8, 5)),
-            pltpu.SemaphoreType.DMA((8, 9)),
-            pltpu.SemaphoreType.DMA,
-            pltpu.SemaphoreType.DMA,
+            pltpu.VMEM((12, 4, 2, 2, 48, 768), BF),
+            pltpu.VMEM((4, 2, 2, 2, 2, 48, 768), BF),
+            *[low] * 14, *[wide] * 3,
+            pltpu.VMEM((4, 4, 2, 2, 48, 768), BF),
+            pltpu.VMEM((8, 4, 2, 48, 768), BF),
+            pltpu.VMEM((6, 3, 2, 48, 768), BF),
+            pltpu.VMEM((6, 3, 2, 48, 768), BF),
+            pltpu.VMEM((6, 48, 768), BF),
+            pltpu.VMEM((2, 3, 48, 768), BF),
+            pltpu.VMEM((2, 3, 48, 768), BF),
+            pltpu.VMEM((2, 4, 48, 768), BF),
+            pltpu.VMEM((6, 48, 768), F32),
+            pltpu.VMEM((4, 2, 2, 2, 8, 128), F32),
+            pltpu.VMEM((8, 768), F32),
+            pltpu.VMEM((3, 24, 256), F32),
+            pltpu.VMEM((3, 24, 256), F32),
+            pltpu.VMEM((4, 24, 256), F32),
+            dma((8, 5)), dma((8, 9)), dma((8, 10)), dma((8, 10)), dma, dma,
+            dma((9,)), dma((9,)), dma((9,)), dma((9,)),
+            pltpu.SemaphoreType.REGULAR,
         ],
-        compiler_params=pltpu.CompilerParams(collective_id=0, has_side_effects=True, vmem_limit_bytes=60 * 2**20),
-    )(m, o)
-
-
-def scatter_kernel(ga_in, gf_in, res, fin, wa, wf, rd, rq, rlw, rrw, rpw, rln, rrn, rpn, send, recv, cs):
-    ca = pltpu.make_async_copy(ga_in, wa, cs.at[0])
-    cf = pltpu.make_async_copy(gf_in, wf, cs.at[1])
-    ca.start()
-    cf.start()
-    k = Place(wa, wf)
-    k.enter()
-    ca.wait()
-    cf.wait()
-    flows = []
-    for f in (6, 7, 5, 4, 3, 2, 1, 0):
-        if f < PAIRS:
-            slots = (rd.at[f], rq.at[f], rpw.at[f], rlw.at[f], rrw.at[f])
-        else:
-            slots = (rd.at[f], rq.at[f], rpn.at[f - PAIRS], rln.at[f - PAIRS], rrn.at[f - PAIRS])
-        flows.append(Scatter(k, f, send, recv, slots, fin.at[f], res))
-    for flow in flows:
-        flow.stages[0]()
-        flow.stages = flow.stages[1:]
-    for stage in weave(flows):
-        stage()
-    for flow in flows:
-        flow.drain()
-
-
-def scatter_all(ga, gf):
-    bf, f32 = jnp.bfloat16, jnp.float32
-    return pl.pallas_call(
-        scatter_kernel,
-        out_shape=(jax.ShapeDtypeStruct((12, 24, 768), f32), jax.ShapeDtypeStruct((8, 48, 768), f32)),
-        in_specs=[pl.BlockSpec(memory_space=pl.ANY)] * 2,
-        out_specs=[pl.BlockSpec(memory_space=pltpu.VMEM)] * 2,
-        scratch_shapes=[
-            pltpu.VMEM((12, 4, 2, 2, 48, 768), bf),
-            pltpu.VMEM((4, 2, 2, 2, 2, 48, 768), bf),
-            pltpu.VMEM((8, 4, 2, 2, 48, 768), bf),
-            pltpu.VMEM((8, 4, 2, 48, 768), bf),
-            pltpu.VMEM((6, 3, 2, 48, 768), bf),
-            pltpu.VMEM((6, 3, 2, 48, 768), bf),
-            pltpu.VMEM((6, 48, 768), bf),
-            pltpu.VMEM((2, 3, 48, 768), bf),
-            pltpu.VMEM((2, 3, 48, 768), bf),
-            pltpu.VMEM((2, 4, 48, 768), bf),
-            pltpu.SemaphoreType.DMA((8, 10)),
-            pltpu.SemaphoreType.DMA((8, 10)),
-            pltpu.SemaphoreType.DMA((2,)),
-        ],
-        compiler_params=pltpu.CompilerParams(collective_id=1, has_side_effects=True, vmem_limit_bytes=60 * 2**20),
-    )(ga, gf)
+        compiler_params=pltpu.CompilerParams(
+            collective_id=0, has_side_effects=True, vmem_limit_bytes=63 * 2**20
+        ),
+    )(lens, hid, mem, cot, masters, outer, gain_tile, spread, owner, bias_row)
+
+
+def simple_program():
+    prog = [("K", 1, ""), ("X", 0, "")]
+    prog += [("G", f, "own") for f in range(8)]
+    prog += [("K", 2, ""), ("K", 3, ""), ("T", 0, "n1")][:2]
+    for name in ("cross", "L1", "R1", "L2", "R2", "L3", "R3"):
+        prog += [("G", f, name) for f in range(6)]
+        if name != "cross":
+            prog += [("G", f, name) for f in (6, 7)]
+    prog += [("G", f, "cross") for f in (6, 7)]
+    prog += [("K", 4, ""), ("K", 5, ""), ("K", 6, ""), ("T", 0, "gain")]
+    prog += [("G", f, "second") for f in range(8)] + [("G", f, "finish") for f in range(8)]
+    prog += [("G", f, "drain") for f in range(8)]
+    task = lambda *names: [("T", 0, n) for n in names]
+    many = lambda name, n: [("T", i, name) for i in range(n)]
+    prog += task("n1", "q1", "k1", "v1") + many("A1", 3) + task("o1", "n2", "k2", "v2", "q2") + many("A2", 3)
+    prog += task("o2", "n3", "begin")
+    for j in range(4):
+        prog += [("T", j, n) for n in ("act", "out", "back", "grads")]
+        if j == 1:
+            prog += [("S", 4, "start")]
+    prog += [("S", f, "start") for f in (5, 6, 7)]
+    prog += task("low", "nb3", "do2", "w7") + many("B2", 3) + task("dn2", "w6")
+    for s in ("core", "half"):
+        prog += [("S", f, s) for f in (4, 5, 6, 7)]
+    prog += [("S", 3, "start")] + task("mg", "w4", "w5") + [("S", 2, "start")]
+    prog += task("nb2", "do1", "w3") + many("B1", 3) + task("dn1", "w2") + [("S", 1, "start")]
+    prog += task("w0", "w1") + [("S", 0, "start")] + task("nb1") + [("R", 0, "")]
+    for s in ("core", "half"):
+        prog += [("S", f, s) for f in (3, 2, 1, 0)]
+    prog += [("S", f, "cross_in") for f in (6, 7)]
+    for s in ("z1", "z2", "z3"):
+        prog += [("S", f, s) for f in SCATTER_ORDER]
+        prog += [("R", int(s[1]), "")]
+    prog += [("S", f, "last") for f in SCATTER_ORDER if f < 6]
+    prog += [("S", f, "finish") for f in SCATTER_ORDER] + [("R", i, "") for i in range(4, 8)]
+    return tuple(prog)
 
 
 def shards_block(
@@ -973,49 +1451,35 @@
     qk_second, value_second, output_second, inner_second, outer_second, gain_second, table_second,
 ):
     axes = ("dp", "fsdp")
-    micro, _, length, width = hidden.shape
     inner4 = inner_master.reshape(24, 4, 768).transpose(1, 0, 2)
     m = jnp.concatenate(
         [qk_master[0:2], value_master[0:1], output_master[0:1], qk_master[3:4], value_master[1:2],
          qk_master[2:3], output_master[1:2], inner4]
     ).reshape(6, 2, 24, 768)
-    wa, wf = gather_all(m, outer_master)
-    wa = wa.reshape(12, 768, 768)
-    gain_full = lax.all_gather(gain_master.astype(jnp.bfloat16), axes, axis=1, tiled=True)
-    gathered = (
-        jnp.stack([wa[0], wa[1], wa[6], wa[4]]),
-        jnp.stack([wa[2], wa[5]]),
-        jnp.stack([wa[3], wa[7]]),
-        jnp.concatenate([wa[8], wa[9], wa[10], wa[11]], axis=1),
-        wf.reshape(3072, 768),
-        gain_full,
-    )
-    onehot = bucket_onehot(length)
-    bias_heads = jnp.einsum("bij,bh->hij", onehot, table_master, precision=highest)
-    stored, produced = forward_pass(
-        gathered, bias_heads, hidden[:, 0], memory[:, 0], target_lengths[:, 0], memory_lengths[:, 0]
-    )
-    grad_terms, score_term, hidden_grad, memory_grad = backward_pass(
-        gathered, bias_heads, stored, cotangent[:, 0], target_lengths[:, 0]
-    )
-    gqk, gv, go, gi, gw, gg = grad_terms
-    ga = jnp.concatenate(
-        [gqk[0:2], gv[0:1], go[0:1], gqk[3:4], gv[1:2], gqk[2:3], go[1:2],
-         gi.reshape(768, 4, 768).transpose(1, 0, 2)]
-    ).astype(jnp.bfloat16).reshape(12, 4, 2, 2, 48, 768)
-    res, fin = scatter_all(ga, gw.astype(jnp.bfloat16).reshape(4, 2, 2, 2, 2, 48, 768))
-    table_grad = jnp.einsum("bij,hij->bh", onehot, score_term, precision=highest)
-    small = lax.psum(jnp.concatenate([gg.reshape(-1), table_grad.reshape(-1)]), axes)
+    gain_tile = jnp.zeros((8, 128), F32).at[:3, :24].set(gain_master)
+    place = jnp.arange(768)
+    spread = (place[None, :] % 24 == jnp.arange(128)[:, None]).astype(BF)
+    owner = (place[None, :] // 24 == jnp.arange(32)[:, None]).astype(F32)
+    by_distance = bucket_onehot(256)[:, :, 0]
+    row = jnp.einsum("bd,bh->hd", by_distance, table_master, precision=highest)
+    bias_row = jnp.zeros((16, 256), F32).at[:HEADS].set(jnp.roll(row[:, ::-1], 1, axis=1))
+    lens = jnp.concatenate([target_lengths[:, 0], memory_lengths[:, 0]])
+    flat = lambda a: a.reshape(512, 768)
+    low_out, hidden_grad, memory_grad, res, last, small = run_layer(
+        simple_program(), lens, flat(hidden), flat(memory), flat(cotangent), m, outer_master,
+        gain_tile, spread, owner, bias_row,
+    )
     device = lax.axis_index(axes)
-    gain_grad = lax.dynamic_slice(small[:2304].reshape(3, 768), (0, 24 * device), (3, 24))
+    gain_grad = lax.dynamic_slice(small[:9].reshape(3, 768), (0, 24 * device), (3, 24))
+    table_grad = jnp.einsum("bd,hd->bh", by_distance, small[9:21, ::-1], precision=highest)
     gradients = (
         jnp.stack([res[0], res[1], res[6], res[4]]),
         jnp.stack([res[2], res[5]]),
         jnp.stack([res[3], res[7]]),
         res[8:12].transpose(1, 0, 2).reshape(24, 3072),
-        fin[6:].reshape(96, 768),
+        last.reshape(96, 768),
         gain_grad,
-        small[2304:].reshape(BUCKETS, HEADS),
+        table_grad,
     )
     masters = (qk_master, value_master, output_master, inner_master, outer_master, gain_master, table_master)
     firsts = (qk_first, value_first, output_first, inner_first, outer_first, gain_first, table_first)
@@ -1024,14 +1488,15 @@
         adam_step(a, b, c, g, rate_matrix if i < 5 else rate_small, weight_decay if i < 5 else 0.0)
         for i, (a, b, c, g) in enumerate(zip(masters, firsts, seconds, gradients))
     ]
+    whole = lambda a: a.reshape(2, 1, 256, 768)
     return (
-        produced[:, None],
-        hidden_grad[:, None],
-        memory_grad[:, None],
+        whole(low_out),
+        whole(hidden_grad),
+        whole(memory_grad),
         *[u[0] for u in updated],
         *[u[1] for u in updated],
         *[u[2] for u in updated],
-        *[u[0].astype(jnp.bfloat16) for u in updated],
+        *[u[0].astype(BF) for u in updated],
     )
 
 

time: 539 us -> 365 us (0.68); the launches traced: 530 us -> 365 us
  Pallas kernels: 217 us -> 337 us
  matrix products: 112 us -> 0.89 us
  blocking collectives: 80.3 us -> 0 us
  local copies, waits for them, and re-layouts: 92.8 us -> 15.7 us
  other arithmetic: 26.7 us -> 9.63 us
    pallas_call x2 -> x1, Pallas kernels: 217 us -> 337 us  [run_layer(): pl.pallas_call(functools.partial(layer_kernel, program), out_shape=(shape...]
    dot_general x44 -> x2, matrix products: 112 us -> 0.89 us  [the longest x1 0.77 us: shards_block(): jnp.einsum('bd,hd->bh', by_distance, small[9:21, ::-1], precision=highest)]
    all_gather x1 -> x0, blocking collectives: 43.2 us -> none  [shards_block(): lax.all_gather(gain_master.astype(jnp.bfloat16), axes, axis=1, tiled=True)]
    psum x1 -> x0, blocking collectives: 37 us -> none  [shards_block(): lax.psum(jnp.concatenate([gg.reshape(-1), table_grad.reshape(-1)]), axes)]
    reshape x14 -> x1, local copies, waits for them, and re-layouts: 22 us -> 0.01 us  [shards_block(): small[:9].reshape(3, 768)]
    convert_element_type x16 -> x0, local copies, waits for them, and re-layouts: 16.6 us -> none  [the longest x1 2.45 us: backward_pass(): grad_mixed = product_transposed(branch, output_full[1]).astype(jnp.bfloat16)]
    unnamed x222 -> x61, local copies, waits for them, and re-layouts: 25.1 us -> 11.7 us
    reduce_sum x5 -> x0, other arithmetic: 11.1 us -> none  [the longest x1 6.9 us: backward_pass(): score_term = jnp.sum(grad_scores.astype(jnp.float32), axis=0)]
where the time goes in v2:
time: 365 us
  Pallas kernels  337 us (92%)
  local copies, waits for them, and re-layouts  15.7 us (4%)
  other arithmetic  9.63 us (3%)
    pallas_call x1, Pallas kernels, run_layer(): pl.pallas_call(functools.partial(layer_kernel, program), out_shape=(shape...  337 us
    unnamed x61, local copies, waits for them, and re-layouts  11.7 us

profile of v2, /device:TPU:0, one launch (start us, length us, event | category | flops | bytes accessed | tf_op | source)
XLA Modules:
  0.0 364.5 jit_solution(11463948084715480781)
XLA Ops:
  0.7 1.3 pad_add_fusion.lens
  2.0 0.9 slice_dynamic-update-slice_fusion
  2.9 0.9 slice_dynamic-update-slice_fusion.6
  3.8 0.9 slice_dynamic-update-slice_fusion.5
  4.7 0.9 slice_dynamic-update-slice_fusion.4
  5.6 0.9 slice_dynamic-update-slice_fusion.3
  6.4 0.9 slice_dynamic-update-slice_fusion.2
  7.3 0.9 slice_dynamic-update-slice_fusion.1
  8.2 1.0 fusion.4
  9.2 0.7 scatter.6.gain_tile
  9.9 0.7 fusion.spread
  10.6 0.7 fusion.8.owner
  11.3 0.1 compare_select_fusion
  11.4 0.1 convolution_bitcast_fusion
  11.5 0.1 slice.129
  11.6 0.1 reverse.2
  11.8 0.7 select_maximum_fusion.bias_row
  12.5 337.3 %shard_map.489 = (bf16[512,768]{1,0:T(8,128)(2,1)}, f32[512,768]{1,0:T(8,128)}, f32[512,768]{1,0:T(8,128)}, f32[12,24,768]{2,1,0:T(8,128)}, f32[2,48,768]{2,1,0:T(8,128)}, /*index=5*/f32[24,256]{1,0:T(8,128)}) custom-call(s32[4]{0:T(128)} %pad_add_fusion.lens, bf16[512,768]{1,0:T(8,128)(2,1)} %bitcast.52, bf16[512,768]{1,0:T(8,128)(2,1)} %bitcast.53, ...), custom_call_target="tpu_custom_call" | custom-call | tf_op jit(solution)/shard_map/pallas_call | solution.py:1373
  349.9 1.2 fusion.37
  351.1 0.9 slice.117
  352.0 2.2 fusion.35
  354.4 1.0 fusion.31
  355.4 1.1 slice_bitcast_fusion
  356.6 1.1 fusion.29
  357.8 1.1 fusion.26
  358.9 0.7 fusion.24
  359.6 0.2 rev.4
  359.7 0.8 fusion.22
  360.5 0.9 copy.79
  361.4 1.1 copy.80
  362.5 0.8 copy-done
  363.4 1.1 copy.81
  (56 shorter events, 0.3 us)
Async XLA Ops:
  0.7 8.6 %copy-start.21 = (f32[3,24]{1,0:T(4,128)S(1)}, f32[3,24]{1,0:T(4,128)}, u32[]{:S(2)}) copy-start(f32[3,24]{1,0:T(4,128)} %param.40) | copy-start | bytes 868
  0.7 10.7 %copy-start.18 = (f32[32,12]{0,1:T(8,128)S(1)}, f32[32,12]{0,1:T(8,128)}, u32[]{:S(2)}) copy-start(f32[32,12]{0,1:T(8,128)} %param.41) | copy-start | bytes 4612
  9.2 3.3 copy-start.2
  349.8 4.4 %copy-start.6 = (f32[2,24,768]{2,1,0:T(8,128)S(1)}, f32[2,24,768]{2,1,0:T(8,128)}, u32[]{:S(2)}) copy-start(f32[2,24,768]{2,1,0:T(8,128)} %param.36) | copy-start | bytes 442372
  349.9 4.4 %copy-start.7 = (f32[2,24,768]{2,1,0:T(8,128)S(1)}, f32[2,24,768]{2,1,0:T(8,128)}, u32[]{:S(2)}) copy-start(f32[2,24,768]{2,1,0:T(8,128)} %param.37) | copy-start | bytes 442372
  349.9 4.4 %copy-start.13 = (f32[2,24,768]{2,1,0:T(8,128)S(1)}, f32[2,24,768]{2,1,0:T(8,128)}, u32[]{:S(2)}) copy-start(f32[2,24,768]{2,1,0:T(8,128)} %param.44) | copy-start | bytes 442372
  349.9 4.4 %copy-start.14 = (f32[2,24,768]{2,1,0:T(8,128)S(1)}, f32[2,24,768]{2,1,0:T(8,128)}, u32[]{:S(2)}) copy-start(f32[2,24,768]{2,1,0:T(8,128)} %param.51) | copy-start | bytes 442372
  349.9 4.4 %copy-start.15 = (f32[2,24,768]{2,1,0:T(8,128)S(1)}, f32[2,24,768]{2,1,0:T(8,128)}, u32[]{:S(2)}) copy-start(f32[2,24,768]{2,1,0:T(8,128)} %param.50) | copy-start | bytes 442372
  349.9 4.4 %copy-start.16 = (f32[2,24,768]{2,1,0:T(8,128)S(1)}, f32[2,24,768]{2,1,0:T(8,128)}, u32[]{:S(2)}) copy-start(f32[2,24,768]{2,1,0:T(8,128)} %param.43) | copy-start | bytes 442372
  354.3 2.2 copy-start.4
  354.3 2.2 copy-start.8
  354.3 2.2 copy-start.9
  355.4 2.3 copy-start.3
  355.4 2.3 copy-start.10
  355.4 2.3 copy-start.11
  355.4 2.3 copy-start.12
  357.7 1.2 copy-start.17
  357.7 1.2 copy-start.22
  357.7 1.2 copy-start.23
  357.7 2.1 copy-start.19
  357.7 2.1 copy-start.20
  357.7 2.8 copy-start.5
  357.7 3.7 %copy-start.1 = (f32[512,768]{1,0:T(8,128)S(1)}, f32[512,768]{1,0:T(8,128)}, u32[]{:S(2)}) copy-start(f32[512,768]{1,0:T(8,128)} %get-tuple-element.62) | copy-start | bytes 4718596
  361.4 2.0 copy-start
